TPU v7x, 256 devices: a whole 4x4x8 slice. The times are simulated.
256 devices in a mesh: section: 4 (over x), tensor: 64 (over y, z, core).
Axes of the slice: x: 4, y: 4, z: 8, core: 2. Of those that a mesh axis runs over, the one named last changes fastest.
Arguments:
- inputs: bfloat16 [128, 8192], P(None, 'tensor'), may hold values from -6 to 6
- target: bfloat16 [128, 8192], P(None, 'tensor'), may hold values from -6 to 6
- norm_gains: float32 [4, 8192], P('section'), may hold values from 0.5 to 1.5
- w_query: bfloat16 [4, 64, 512, 2048], P('section', 'tensor'), may hold values from -0.0625 to 0.0625
- w_keyval: bfloat16 [4, 64, 512, 512], P('section', 'tensor'), may hold values from -0.0625 to 0.0625
- w_output: bfloat16 [4, 64, 2048, 512], P('section', 'tensor'), may hold values from -0.0625 to 0.0625
- noise_seed: int32 [1], replicated, may hold values from 0 to 999999
- step_count: int32 [1], replicated, may hold values from 0 to 99999
Outputs:
- layer_outputs: bfloat16 [4, 2, 128, 8192], P('section', None, None, 'tensor')
- losses: float32 [4, 2], P('section')
- new_gains: float32 [4, 8192], P('section')
- new_query: bfloat16 [4, 64, 512, 2048], P('section', 'tensor')
- new_keyval: bfloat16 [4, 64, 512, 512], P('section', 'tensor')
- new_output: bfloat16 [4, 64, 2048, 512], P('section', 'tensor')
All inputs are finite; a program needn't handle non-finite values.
Results may differ from a plain program's by a relative error of at most 0.01.
Values may be sent and summed in bfloat16 or wider, within the bound.
No kernel may reach another device: no remote copies, remote signals or barrier semaphores. Data moves between devices by JAX's collectives and lax.ppermute only.
A program may use at most 64 MiB of HBM per device.

v0:
```python
import functools

import jax
import jax.numpy as jnp
import numpy as np
from jax import lax
from jax.experimental import pallas as pl
from jax.experimental.pallas import tpu as pltpu
from jax.sharding import Mesh, PartitionSpec as P

HD = 128
NY, NZ, NC = 4, 8, 2
LANE = 128

perturb_scale = 0.001
learn_rate = 1e-05
rope_base = 500000.0


def logical(value, by):
    return lax.shift_right_logical(value, jnp.full(value.shape, by, value.dtype))


def mix_bits(hashed):
    hashed = hashed ^ logical(hashed, 16)
    hashed = hashed * jnp.int32(2146121005)
    hashed = hashed ^ logical(hashed, 15)
    hashed = hashed * jnp.int32(-2073254261)
    hashed = hashed ^ logical(hashed, 16)
    return hashed


def noise_of(index, salt):
    hashed = mix_bits(mix_bits(index ^ salt) + salt)
    uniform_part = logical(hashed, 8).astype(jnp.float32) * (1.0 / 16777216.0)
    return (uniform_part - 0.5) * 3.4641016


def limit(mib):
    return pltpu.CompilerParams(vmem_limit_bytes=mib * 1024 * 1024)


def perturb_input_kernel(full, spread, groups, ints_ref, sign_ref, q_ref, k_ref, zq_ref, zk_ref, mine_ref, other_ref):
    rows, query_cols = q_ref.shape
    keyval_cols = k_ref.shape[1]
    row = lax.broadcasted_iota(jnp.int32, (rows, 1), 0) + pl.program_id(0) * spread + ints_ref[2]
    for w_ref, z_ref, at, salt, cols, first in (
        (q_ref, zq_ref, 0, ints_ref[0], full, ints_ref[3]),
        (k_ref, zk_ref, query_cols, ints_ref[1], keyval_cols * groups, ints_ref[4]),
    ):
        width = w_ref.shape[1]
        col = lax.broadcasted_iota(jnp.int32, (1, width), 1) + first
        z = noise_of(row * cols + col, salt)
        z_ref[...] = z
        w = w_ref[...].astype(jnp.float32)
        shift = sign_ref[0] * z
        mine_ref[:, at : at + width] = (w + shift).astype(jnp.bfloat16)
        other_ref[:, at : at + width] = (w - shift).astype(jnp.bfloat16)


def perturb_output_kernel(full, spread, width, ints_ref, sign_ref, w_ref, z_ref, mine_ref, other_ref):
    rows, cols = w_ref.shape
    row = lax.broadcasted_iota(jnp.int32, (rows, 1), 0) + pl.program_id(0) * rows + ints_ref[1]
    col = lax.broadcasted_iota(jnp.int32, (1, cols), 1)
    col = col + col // width * (spread - width) + ints_ref[2]
    z = noise_of(row * full + col, ints_ref[0])
    z_ref[...] = z
    w = w_ref[...].astype(jnp.float32)
    shift = sign_ref[0] * z
    mine_ref[...] = (w + shift).astype(jnp.bfloat16)
    other_ref[...] = (w - shift).astype(jnp.bfloat16)


def update_kernel(rate_ref, *refs):
    count = len(refs) // 3
    for w_ref, z_ref, out_ref in zip(refs[:count], refs[count : 2 * count], refs[2 * count :]):
        out_ref[...] = (w_ref[...].astype(jnp.float32) - rate_ref[0] * z_ref[...]).astype(jnp.bfloat16)


def by_rows(array, steps):
    return pl.BlockSpec((array.shape[0] // steps, array.shape[1]), lambda i: (i, 0))


def noise_cost(count):
    return pl.CostEstimate(flops=60 * count, bytes_accessed=10 * count, transcendentals=0)


def shifted(array, axis, count, by):
    return lax.ppermute(array, axis, [(i, (i + by) % count) for i in range(count)])


def swapped(array):
    return lax.ppermute(array, "core", [(0, 1), (1, 0)])


def rope_tables(tokens):
    half = HD // 2
    frequency = np.float32(rope_base) ** (-np.arange(half, dtype=np.float32) * np.float32(2.0) / np.float32(HD))
    angles = np.arange(tokens, dtype=np.float32)[:, None] * frequency.astype(np.float32)[None, :]
    cosine = np.cos(angles.astype(np.float64)).astype(np.float32)
    sine = np.sin(angles.astype(np.float64)).astype(np.float32)
    return np.concatenate([cosine, cosine], 1), np.concatenate([-sine, sine], 1)


def rotate(values, cosine, sine):
    return values * cosine + pltpu.roll(values, HD // 2, 1) * sine


def same_index(size):
    return lax.broadcasted_iota(jnp.int32, (size, size), 0) == lax.broadcasted_iota(
        jnp.int32, (size, size), 1
    )


def project_kernel(y_ref, *refs):
    around = refs[:NY]
    gains_ref, mine, part, out_ref, scaled = refs[NY:]
    tokens, width = around[0].shape[1:]
    total = jnp.zeros((tokens, 1), jnp.float32)
    for k in range(NY):
        place = pl.multiple_of(lax.rem(y_ref[0] + (NY - k), NY) * width, width)
        for half in range(NC):
            wide = around[k][half].astype(jnp.float32)
            total = total + jnp.sum(wide * wide, axis=1, keepdims=True)
            scaled[half, :, pl.ds(place, width)] = (wide * gains_ref[half, k : k + 1, :]).astype(jnp.bfloat16)

    def product(start, size):
        return jnp.dot(
            scaled[0], mine[:, start : start + size], preferred_element_type=jnp.float32
        ) + jnp.dot(scaled[1], part[:, start : start + size], preferred_element_type=jnp.float32)

    kept = out_ref.shape[1] - 16 - 2 * tokens
    span = kept // tokens * HD
    for dest in range(NZ):
        query = product(dest * span, span).astype(jnp.bfloat16)
        for head in range(span // HD):
            out_ref[dest, head * tokens : (head + 1) * tokens, :] = query[:, head * HD : (head + 1) * HD]
    groups = (mine.shape[1] - NZ * span) // (2 * HD)
    for group in range(groups):
        keyval = product(NZ * span + group * 2 * HD, 2 * HD).astype(jnp.bfloat16)
        for dest in range(group * NZ // groups, (group + 1) * NZ // groups):
            out_ref[dest, kept : kept + tokens, :] = keyval[:, :HD]
            out_ref[dest, kept + tokens : kept + 2 * tokens, :] = keyval[:, HD:]
    row = jnp.sum(jnp.where(same_index(tokens), total, 0.0), axis=0, keepdims=True)
    high = row.astype(jnp.bfloat16).astype(jnp.float32)
    line = lax.broadcasted_iota(jnp.int32, (16, tokens), 0)
    extra = jnp.where(line == 0, high, jnp.where(line == 1, row - high, 0.0)).astype(jnp.bfloat16)
    for dest in range(NZ):
        out_ref[dest, kept + 2 * tokens :, :] = extra


def attend_kernel(full, recv_ref, cos_ref, sin_ref, out_ref):
    tokens = cos_ref.shape[0]
    heads = out_ref.shape[1] // tokens

    def total(start, size):
        acc = recv_ref[0, start : start + size, :].astype(jnp.float32)
        for source in range(1, NZ):
            acc = acc + recv_ref[source, start : start + size, :].astype(jnp.float32)
        return acc

    cosine = cos_ref[...]
    sine = sin_ref[...]
    kept = heads * tokens
    squares = total(kept + 2 * tokens, 16)
    row = squares[0:1] + squares[1:2]
    column = jnp.sum(jnp.where(same_index(tokens), row, 0.0), axis=1, keepdims=True)
    inverse = lax.rsqrt(column / full + 1e-05)
    key = (total(kept, tokens) * inverse).astype(jnp.bfloat16).astype(jnp.float32)
    key = rotate(key, cosine, sine)
    value = (total(kept + tokens, tokens) * inverse).astype(jnp.bfloat16)
    causal = lax.broadcasted_iota(jnp.int32, (tokens, tokens), 0) >= lax.broadcasted_iota(
        jnp.int32, (tokens, tokens), 1
    )
    for head in range(heads):
        query = rotate(total(head * tokens, tokens) * inverse, cosine, sine)
        scores = lax.dot_general(
            query, key, (((1,), (1,)), ((), ())),
            precision=lax.Precision.HIGHEST, preferred_element_type=jnp.float32,
        ) * (1.0 / np.sqrt(np.float32(HD)))
        expo = jnp.where(causal, jnp.exp(scores), 0.0)
        weights = (expo / jnp.sum(expo, axis=1, keepdims=True)).astype(jnp.bfloat16)
        mixed = jnp.dot(weights, value, preferred_element_type=jnp.float32).astype(jnp.bfloat16)
        for dest in range(NZ):
            out_ref[dest, head * tokens : (head + 1) * tokens, :] = mixed


def output_kernel(y_ref, heads_ref, o_mine, o_part, hidden_ref, base_ref, *refs):
    sent = refs[: NY - 1]
    joined, pieces = refs[NY - 1 :]
    tokens, width = hidden_ref.shape[1:]
    for source in range(heads_ref.shape[0]):
        for head in range(heads_ref.shape[1] // tokens):
            at = (source * (heads_ref.shape[1] // tokens) + head) * HD
            joined[:, at : at + HD] = heads_ref[source, head * tokens : (head + 1) * tokens, :]
    for half, weight in enumerate((o_mine, o_part)):
        for pair in range(NY // 2):
            at = pair * 2 * width
            product = jnp.dot(
                joined[...], weight[:, at : at + 2 * width], preferred_element_type=jnp.float32
            )
            for inner in range(2):
                step = lax.rem(pair * 2 + inner + NY - y_ref[0], NY)
                pieces[step, half] = product[:, inner * width : (inner + 1) * width]
    base_ref[...] = hidden_ref[...].astype(jnp.float32) + pieces[0]
    for k in range(1, NY):
        sent[k - 1][...] = pieces[k].astype(jnp.bfloat16)


VMEM = pl.BlockSpec(memory_space=pltpu.VMEM)
SMEM = pl.BlockSpec(memory_space=pltpu.SMEM)


def summed_over(value, axis, steps):
    count = lax.axis_size(axis)
    got = [
        lax.ppermute(value, axis, [(i, i ^ step) for i in range(count)]) for step in steps
    ]
    if len(got) == 1:
        return value + got[0]
    return (value + got[0]) + (got[1] + got[2])


def local(inputs, target, norm_gains, w_query, w_keyval, w_output, noise_seed, step_count):
    section = lax.axis_index("section")
    sections = lax.axis_size("section")
    y = lax.axis_index("y")
    z = lax.axis_index("z")
    core = lax.axis_index("core")
    tokens, width = inputs.shape
    full = width * NY * NZ * NC
    query_cols = w_query.shape[3]
    keyval_cols = w_keyval.shape[3]
    block = z * NC + core
    amount = jnp.where(core == 0, perturb_scale, -perturb_scale).astype(jnp.float32)
    spread = NZ * NC * width

    def salt(code):
        return mix_bits(mix_bits(step_count[0] * 40503 + (4 * section + code) * 1000003) ^ noise_seed[0])

    wq, wk, wo = w_query[0, 0], w_keyval[0, 0], w_output[0, 0]
    paired = jax.ShapeDtypeStruct((wq.shape[0], query_cols + keyval_cols), jnp.bfloat16)
    zq, zk, in_mine, in_other = pl.pallas_call(
        functools.partial(perturb_input_kernel, full, spread, NY),
        grid=(NY,),
        in_specs=[SMEM, SMEM, by_rows(wq, NY), by_rows(wk, NY)],
        out_specs=[by_rows(wq, NY), by_rows(wk, NY), by_rows(paired, NY), by_rows(paired, NY)],
        out_shape=[
            jax.ShapeDtypeStruct(wq.shape, jnp.float32),
            jax.ShapeDtypeStruct(wk.shape, jnp.float32),
            paired,
            paired,
        ],
        compiler_params=limit(14),
        cost_estimate=noise_cost(wq.size + wk.size),
    )(
        jnp.stack([salt(1), salt(2), block * width, y * query_cols, y * keyval_cols]),
        amount.reshape(1), wq, wk,
    )
    in_part = swapped(in_other)
    hidden = jnp.stack([inputs, swapped(inputs)])
    around = [hidden] + [shifted(hidden, "y", NY, k) for k in range(1, NY)]
    wo, around[1] = lax.optimization_barrier((wo, around[1]))
    zo, o_mine, o_other = pl.pallas_call(
        functools.partial(perturb_output_kernel, full, spread, width),
        grid=(8,),
        in_specs=[SMEM, SMEM, by_rows(wo, 8)],
        out_specs=[by_rows(wo, 8)] * 3,
        out_shape=[
            jax.ShapeDtypeStruct(wo.shape, jnp.float32),
            jax.ShapeDtypeStruct(wo.shape, jnp.bfloat16),
            jax.ShapeDtypeStruct(wo.shape, jnp.bfloat16),
        ],
        compiler_params=limit(14),
        cost_estimate=noise_cost(wo.size),
    )(
        jnp.stack([salt(3), y * query_cols, block * width]),
        amount.reshape(1), wo,
    )
    o_part = swapped(o_other)
    in_mine, o_mine = lax.optimization_barrier((in_mine, o_mine))

    gain_noise = noise_of(jnp.arange(full, dtype=jnp.int32), salt(0))
    gains = (norm_gains[0] + amount * gain_noise).reshape(NY, NZ, NC, width)
    gains = lax.dynamic_index_in_dim(gains, z, 1, keepdims=False)
    gains = jnp.where(core == 0, gains, gains[:, ::-1])
    gains = jnp.take(gains.transpose(1, 0, 2), (y - jnp.arange(NY)) % NY, axis=1)

    cosine, sine = (jnp.asarray(t) for t in rope_tables(tokens))
    place = y.reshape(1)
    heads_z = query_cols // HD // NZ
    rows = (heads_z + 2) * tokens + 16

    def project(around):
        return pl.pallas_call(
            project_kernel,
            in_specs=[SMEM] + [VMEM] * (NY + 3),
            out_specs=VMEM,
            out_shape=jax.ShapeDtypeStruct((NZ, rows, HD), jnp.bfloat16),
            scratch_shapes=[pltpu.VMEM((NC, tokens, NY * width), jnp.bfloat16)],
            compiler_params=limit(14),
        )(place, *around, gains, in_mine, in_part)

    def attend(received):
        return pl.pallas_call(
            functools.partial(attend_kernel, full),
            in_specs=[VMEM] * 3,
            out_specs=VMEM,
            out_shape=jax.ShapeDtypeStruct((NZ, heads_z * tokens, HD), jnp.bfloat16),
            compiler_params=limit(14),
        )(received, cosine, sine)

    def output(heads, hidden):
        return pl.pallas_call(
            output_kernel,
            in_specs=[SMEM] + [VMEM] * 4,
            out_specs=[VMEM] * NY,
            out_shape=[jax.ShapeDtypeStruct(hidden.shape, jnp.float32)]
            + [jax.ShapeDtypeStruct(hidden.shape, jnp.bfloat16)] * (NY - 1),
            scratch_shapes=[
                pltpu.VMEM((tokens, query_cols), jnp.bfloat16),
                pltpu.VMEM((NY,) + hidden.shape, jnp.float32),
            ],
            compiler_params=limit(14),
        )(place, heads, o_mine, o_part, hidden)

    goal = jnp.stack([target, swapped(target)])
    record = jnp.zeros_like(hidden)
    for tick in range(4):
        if tick:
            around = [hidden] + [shifted(hidden, "y", NY, k) for k in range(1, NY)]
        received = lax.all_to_all(project(around), "z", 0, 0, tiled=True)
        heads = lax.all_to_all(attend(received), "z", 0, 0, tiled=True)
        base, *pieces = output(heads, hidden)
        for k in range(1, NY):
            base = base + shifted(pieces[k - 1], "y", NY, k).astype(jnp.float32)
        result = base.astype(jnp.bfloat16)
        record = jnp.where(section == tick, result, record)
        if tick < 3:
            hidden = lax.ppermute(result, "section", [(tick, tick + 1)])

    gap = result.astype(jnp.float32) - goal.astype(jnp.float32)
    squared = jnp.sum(gap * gap)
    squared = jnp.full((8, LANE), squared)
    squared = summed_over(squared, "y", (1, 2, 3))
    squared = summed_over(squared, "z", (1,))
    squared = summed_over(squared, "z", (2, 4, 6))
    copies = [lax.ppermute(squared, "section", [(sections - 1, k)]) for k in range(sections - 1)]
    squared = jnp.where(section == sections - 1, squared, sum(copies[1:], copies[0]))
    partner = swapped(squared)
    squared = jnp.where(core == 0, jnp.stack([squared, partner]), jnp.stack([partner, squared]))[:, 0, 0]
    losses = squared / (tokens * full)
    rate = learn_rate * ((losses[0] - losses[1]) / (2.0 * perturb_scale))
    new_gains = (norm_gains[0] - rate * gain_noise)[None]

    arrays = (wq, wk, wo)
    specs = [by_rows(w, 8) for w in arrays]
    new_query, new_keyval, new_output = pl.pallas_call(
        update_kernel,
        grid=(8,),
        in_specs=[SMEM] + specs + specs,
        out_specs=specs,
        out_shape=[jax.ShapeDtypeStruct(w.shape, jnp.bfloat16) for w in arrays],
        compiler_params=limit(14),
    )(rate.reshape(1), *arrays, zq, zk, zo)
    mine, other = record[0], swapped(record[1])
    layer_outputs = jnp.where(core == 0, jnp.stack([mine, other]), jnp.stack([other, mine]))[None]
    return (
        layer_outputs,
        losses[None],
        new_gains,
        new_query[None, None],
        new_keyval[None, None],
        new_output[None, None],
    )


def solution(mesh):
    mesh = Mesh(mesh.devices.reshape(-1, NY, NZ, NC), ("section", "y", "z", "core"))
    tensor = ("y", "z", "core")
    return jax.shard_map(
        local,
        mesh=mesh,
        in_specs=(
            P(None, tensor),
            P(None, tensor),
            P("section", None),
            P("section", tensor, None, None),
            P("section", tensor, None, None),
            P("section", tensor, None, None),
            P(),
            P(),
        ),
        out_specs=(
            P("section", None, None, tensor),
            P("section", None),
            P("section", None),
            P("section", tensor, None, None),
            P("section", tensor, None, None),
            P("section", tensor, None, None),
        ),
        check_vma=False,
    )
```

profile of v0, /device:TPU:5, one launch (start us, length us, event | category | flops | bytes accessed | tf_op | source)
XLA Modules:
  0.0 376.7 jit_solution(12765859452938625440)
XLA Ops:
  4.7 6.8 %shard_map.145 = (f32[512,2048]{1,0:T(8,128)S(1)}, f32[512,512]{1,0:T(8,128)S(1)}, bf16[512,2560]{1,0:T(8,128)(2,1)S(1)}, bf16[512,2560]{1,0:T(8,128)(2,1)}) custom-call(s32[5]{0:T(128)S(1)} %stack.78.ints_ref, f32[1]{0:T(128)} %bitcast.16.sign_ref, bf16[512,2048]{1,0:T(8,128)(2,1)S(1)} %bitcast.42, bf16[512,512]{1,0:T(8,128)(2,1)S(1)} %bitcast.46), custom_call_target="tpu_custom_call" | custom-call | flops 78643200 | bytes 13107200 | tf_op jit(solution)/shard_map/pallas_call | solution.py:243
  15.9 3.6 collective-permute-done
  26.3 5.0 %shard_map.146 = (f32[2048,512]{1,0:T(8,128)S(1)}, bf16[2048,512]{1,0:T(8,128)(2,1)S(1)}, bf16[2048,512]{1,0:T(8,128)(2,1)S(1)}) custom-call(s32[3]{0:T(128)S(1)} %pad_add_fusion.ints_ref, f32[1]{0:T(128)} %bitcast.16.sign_ref, bf16[2048,512]{1,0:T(8,128)(2,1)S(1)} %bitcast.44), custom_call_target="tpu_custom_call" | custom-call | flops 62914560 | bytes 10485760 | tf_op jit(solution)/shard_map/pallas_call | solution.py:264
  36.0 2.7 shard_map.147
  39.7 8.3 %all-to-all-start = ((bf16[8,528,128]{2,1,0:T(8,128)(2,1)}), bf16[8,528,128]{2,1,0:T(8,128)(2,1)}, u32[]{:S(2)}, u32[]{:S(2)}) async-start(bf16[8,528,128]{2,1,0:T(8,128)(2,1)} %copy-done.7), calls=%async_computation | async-start | bytes 2162688 | tf_op jit(solution)/shard_map/all_to_all | solution.py:332
  49.2 28.8 %all-to-all-done.recv_ref = bf16[8,528,128]{2,1,0:T(8,128)(2,1)} async-done(((bf16[8,528,128]{2,1,0:T(8,128)(2,1)}), bf16[8,528,128]{2,1,0:T(8,128)(2,1)}, u32[]{:S(2)}, u32[]{:S(2)}) %all-to-all-start) | async-done | bytes 1081376 | tf_op jit(solution)/shard_map/all_to_all | solution.py:332
  81.2 3.5 all-to-all-start.1
  84.7 17.9 %all-to-all-done.1.heads_ref = bf16[8,256,128]{2,1,0:T(8,128)(2,1)S(1)} async-done(((bf16[8,256,128]{2,1,0:T(8,128)(2,1)}), bf16[8,256,128]{2,1,0:T(8,128)(2,1)S(1)}, u32[]{:S(2)}, u32[]{:S(2)}) %all-to-all-start.1) | async-done | bytes 524320 | tf_op jit(solution)/shard_map/all_to_all | solution.py:333
  114.5 3.0 collective-permute-start.11
  123.7 28.4 %all_to_all.40.recv_ref = bf16[8,528,128]{2,1,0:T(8,128)(2,1)S(1)} all-to-all(bf16[8,528,128]{2,1,0:T(8,128)(2,1)S(1)} %shard_map.150), channel_id=1, replica_groups=mesh['section'=4,'y'=4,'z'=8,'core'=2] {'z'}, dimensions={0} | all-to-all | bytes 2162688 | tf_op jit(solution)/shard_map/all_to_all | solution.py:332
  153.3 16.0 %all_to_all.41.heads_ref = bf16[8,256,128]{2,1,0:T(8,128)(2,1)S(1)} all-to-all(bf16[8,256,128]{2,1,0:T(8,128)(2,1)S(1)} %shard_map.151), channel_id=1, replica_groups=mesh['section'=4,'y'=4,'z'=8,'core'=2] {'z'}, dimensions={0} | all-to-all | bytes 1048576 | tf_op jit(solution)/shard_map/all_to_all | solution.py:333
  178.8 4.6 %collective-permute-done.16.refs_0_.hidden_ref = bf16[2,128,128]{2,1,0:T(8,128)(2,1)S(1)} collective-permute-done((bf16[2,128,128]{2,1,0:T(8,128)(2,1)S(1)}, bf16[2,128,128]{2,1,0:T(8,128)(2,1)S(1)}, u32[]{:S(2)}, u32[]{:S(2)}) %collective-permute-start.16) | collective-permute-done | bytes 65568 | tf_op jit(solution)/shard_map/ppermute | solution.py:340
  184.5 3.0 collective-permute-start.18
  193.6 20.2 %all_to_all.42.recv_ref = bf16[8,528,128]{2,1,0:T(8,128)(2,1)S(1)} all-to-all(bf16[8,528,128]{2,1,0:T(8,128)(2,1)S(1)} %shard_map.153), channel_id=1, replica_groups=mesh['section'=4,'y'=4,'z'=8,'core'=2] {'z'}, dimensions={0} | all-to-all | bytes 2162688 | tf_op jit(solution)/shard_map/all_to_all | solution.py:332
  214.9 16.4 %all_to_all.43.heads_ref = bf16[8,256,128]{2,1,0:T(8,128)(2,1)S(1)} all-to-all(bf16[8,256,128]{2,1,0:T(8,128)(2,1)S(1)} %shard_map.154), channel_id=1, replica_groups=mesh['section'=4,'y'=4,'z'=8,'core'=2] {'z'}, dimensions={0} | all-to-all | bytes 1048576 | tf_op jit(solution)/shard_map/all_to_all | solution.py:333
  242.4 9.1 %collective-permute-start.24 = (bf16[2,128,128]{2,1,0:T(8,128)(2,1)S(1)}, bf16[2,128,128]{2,1,0:T(8,128)(2,1)S(1)}, u32[]{:S(2)}, u32[]{:S(2)}) collective-permute-start(bf16[2,128,128]{2,1,0:T(8,128)(2,1)S(1)} %collective-permute-done.23.refs_0_.hidden_ref), channel_id=1, source_target_pairs={{0,16},{16,32},{32,48},{48,0},{1,17},{17,33},{33,49},{49,1},{2,18}... | collective-permute-start | bytes 196616 | tf_op jit(solution)/shard_map/ppermute | solution.py:89
  251.5 2.8 collective-permute-start.25
  260.1 20.5 %all_to_all.44.recv_ref = bf16[8,528,128]{2,1,0:T(8,128)(2,1)S(1)} all-to-all(bf16[8,528,128]{2,1,0:T(8,128)(2,1)S(1)} %shard_map.156), channel_id=1, replica_groups=mesh['section'=4,'y'=4,'z'=8,'core'=2] {'z'}, dimensions={0} | all-to-all | bytes 2162688 | tf_op jit(solution)/shard_map/all_to_all | solution.py:332
  281.7 20.9 %all_to_all.45.heads_ref = bf16[8,256,128]{2,1,0:T(8,128)(2,1)S(1)} all-to-all(bf16[8,256,128]{2,1,0:T(8,128)(2,1)S(1)} %shard_map.157), channel_id=1, replica_groups=mesh['section'=4,'y'=4,'z'=8,'core'=2] {'z'}, dimensions={0} | all-to-all | bytes 1048576 | tf_op jit(solution)/shard_map/all_to_all | solution.py:333
  309.0 18.1 %collective-permute-start.31 = (bf16[128,128]{1,0:T(8,128)(2,1)S(1)}, bf16[128,128]{1,0:T(8,128)(2,1)S(1)}, u32[]{:S(2)}, u32[]{:S(2)}) collective-permute-start(bf16[128,128]{1,0:T(8,128)(2,1)S(1)} %copy-done.21), channel_id=1, source_target_pairs={{0,1},{1,0},{2,3},{3,2},{4,5},{5,4},{6,7},{7,6},{8,9},{9,8},{10,11... | collective-permute-start | bytes 98312 | tf_op jit(solution)/shard_map/ppermute | solution.py:93
  340.2 3.6 collective-permute-start.38
  347.5 4.6 %collective-permute-done.41 = f32[8,128]{1,0:T(8,128)S(1)} collective-permute-done((f32[8,128]{1,0:T(8,128)S(1)}, f32[8,128]{1,0:T(8,128)S(1)}, u32[]{:S(2)}, u32[]{:S(2)}) %collective-permute-start.41) | collective-permute-done | bytes 4128 | tf_op jit(solution)/shard_map/ppermute | solution.py:348
  352.0 8.8 %collective-permute-start.42 = (f32[8,128]{1,0:T(8,128)S(1)}, f32[8,128]{1,0:T(8,128)S(1)}, u32[]{:S(2)}, u32[]{:S(2)}) collective-permute-start(f32[8,128]{1,0:T(8,128)S(1)} %add_select_fusion), channel_id=1, source_target_pairs={{0,1},{1,0},{2,3},{3,2},{4,5},{5,4},{6,7},{7,6},{8,9},{9,8},{10,11... | collective-permute-start | bytes 12296 | tf_op jit(solution)/shard_map/ppermute | solution.py:93
  372.1 3.7 shard_map.159
  (161 shorter events, 112.6 us)
Async XLA Ops:
  14.4 21.6 %collective-permute-start.4 = (bf16[512,2560]{1,0:T(8,128)(2,1)}, bf16[512,2560]{1,0:T(8,128)(2,1)}, u32[]{:S(2)}, u32[]{:S(2)}) collective-permute-start(bf16[512,2560]{1,0:T(8,128)(2,1)} %get-tuple-element.41), channel_id=1, source_target_pairs={{0,1},{1,0},{2,3},{3,2},{4,5},{5,4},{6,7},{7,6},{8,9},{9,8},{10,11... | collective-permute-start | bytes 7864328 | tf_op jit(solution)/shard_map/ppermute | solution.py:93
  19.6 5.1 %collective-permute-start.1 = (bf16[2,128,128]{2,1,0:T(8,128)(2,1)S(1)}, bf16[2,128,128]{2,1,0:T(8,128)(2,1)S(1)}, u32[]{:S(2)}, u32[]{:S(2)}) collective-permute-start(bf16[2,128,128]{2,1,0:T(8,128)(2,1)S(1)} %pad_maximum_fusion.refs_0_.hidden_ref), channel_id=1, source_target_pairs={{0,16},{16,32},{32,48},{48,0},{1,17},{17,33},{33,49},{49,1},{2,18}... | collective-permute-start | bytes 196616 | tf_op jit(solution)/shard_map/ppermute | solution.py:89
  21.0 15.1 %collective-permute-start.2 = (bf16[2,128,128]{2,1,0:T(8,128)(2,1)S(1)}, bf16[2,128,128]{2,1,0:T(8,128)(2,1)S(1)}, u32[]{:S(2)}, u32[]{:S(2)}) collective-permute-start(bf16[2,128,128]{2,1,0:T(8,128)(2,1)S(1)} %pad_maximum_fusion.refs_0_.hidden_ref), channel_id=1, source_target_pairs={{0,32},{16,48},{32,0},{48,16},{1,33},{17,49},{33,1},{49,17},{2,34}... | collective-permute-start | bytes 196616 | tf_op jit(solution)/shard_map/ppermute | solution.py:89
  23.6 12.4 %collective-permute-start.3 = (bf16[2,128,128]{2,1,0:T(8,128)(2,1)S(1)}, bf16[2,128,128]{2,1,0:T(8,128)(2,1)S(1)}, u32[]{:S(2)}, u32[]{:S(2)}) collective-permute-start(bf16[2,128,128]{2,1,0:T(8,128)(2,1)S(1)} %pad_maximum_fusion.refs_0_.hidden_ref), channel_id=1, source_target_pairs={{0,48},{16,0},{32,16},{48,32},{1,49},{17,1},{33,17},{49,33},{2,50}... | collective-permute-start | bytes 196616 | tf_op jit(solution)/shard_map/ppermute | solution.py:89
  39.7 38.3 %all-to-all-start = ((bf16[8,528,128]{2,1,0:T(8,128)(2,1)}), bf16[8,528,128]{2,1,0:T(8,128)(2,1)}, u32[]{:S(2)}, u32[]{:S(2)}) async-start(bf16[8,528,128]{2,1,0:T(8,128)(2,1)} %copy-done.7), calls=%async_computation | async-start | bytes 2162688 | tf_op jit(solution)/shard_map/all_to_all | solution.py:332
  48.0 36.7 %collective-permute-start.5 = (bf16[2048,512]{1,0:T(8,128)(2,1)}, bf16[2048,512]{1,0:T(8,128)(2,1)}, u32[]{:S(2)}, u32[]{:S(2)}) collective-permute-start(bf16[2048,512]{1,0:T(8,128)(2,1)} %copy-done.19), channel_id=1, source_target_pairs={{0,1},{1,0},{2,3},{3,2},{4,5},{5,4},{6,7},{7,6},{8,9},{9,8},{10,11... | collective-permute-start | bytes 6291464 | tf_op jit(solution)/shard_map/ppermute | solution.py:93
  81.2 21.4 %all-to-all-start.1 = ((bf16[8,256,128]{2,1,0:T(8,128)(2,1)}), bf16[8,256,128]{2,1,0:T(8,128)(2,1)S(1)}, u32[]{:S(2)}, u32[]{:S(2)}) async-start(bf16[8,256,128]{2,1,0:T(8,128)(2,1)} %copy-done.14), calls=%async_computation.1 | async-start | bytes 1048576 | tf_op jit(solution)/shard_map/all_to_all | solution.py:333
  107.1 5.2 %collective-permute-start.7 = (bf16[2,128,128]{2,1,0:T(8,128)(2,1)S(1)}, bf16[2,128,128]{2,1,0:T(8,128)(2,1)S(1)}, u32[]{:S(2)}, u32[]{:S(2)}) collective-permute-start(bf16[2,128,128]{2,1,0:T(8,128)(2,1)S(1)} %get-tuple-element.46), channel_id=1, source_target_pairs={{0,32},{16,48},{32,0},{48,16},{1,33},{17,49},{33,1},{49,17},{2,34}... | collective-permute-start | bytes 196616 | tf_op jit(solution)/shard_map/ppermute | solution.py:89
  114.5 5.1 %collective-permute-start.11 = (bf16[2,128,128]{2,1,0:T(8,128)(2,1)S(1)}, bf16[2,128,128]{2,1,0:T(8,128)(2,1)S(1)}, u32[]{:S(2)}, u32[]{:S(2)}) collective-permute-start(bf16[2,128,128]{2,1,0:T(8,128)(2,1)S(1)} %collective-permute-done.9.refs_0_.hidden_ref), channel_id=1, source_target_pairs={{0,32},{16,48},{32,0},{48,16},{1,33},{17,49},{33,1},{49,17},{2,34}... | collective-permute-start | bytes 196616 | tf_op jit(solution)/shard_map/ppermute | solution.py:89
  171.8 5.1 %collective-permute-start.13 = (bf16[2,128,128]{2,1,0:T(8,128)(2,1)S(1)}, bf16[2,128,128]{2,1,0:T(8,128)(2,1)S(1)}, u32[]{:S(2)}, u32[]{:S(2)}) collective-permute-start(bf16[2,128,128]{2,1,0:T(8,128)(2,1)S(1)} %get-tuple-element.49), channel_id=1, source_target_pairs={{0,16},{16,32},{32,48},{48,0},{1,17},{17,33},{33,49},{49,1},{2,18}... | collective-permute-start | bytes 196616 | tf_op jit(solution)/shard_map/ppermute | solution.py:89
  171.8 5.0 %collective-permute-start.14 = (bf16[2,128,128]{2,1,0:T(8,128)(2,1)S(1)}, bf16[2,128,128]{2,1,0:T(8,128)(2,1)S(1)}, u32[]{:S(2)}, u32[]{:S(2)}) collective-permute-start(bf16[2,128,128]{2,1,0:T(8,128)(2,1)S(1)} %get-tuple-element.50), channel_id=1, source_target_pairs={{0,32},{16,48},{32,0},{48,16},{1,33},{17,49},{33,1},{49,17},{2,34}... | collective-permute-start | bytes 196616 | tf_op jit(solution)/shard_map/ppermute | solution.py:89
  177.5 5.9 %collective-permute-start.16 = (bf16[2,128,128]{2,1,0:T(8,128)(2,1)S(1)}, bf16[2,128,128]{2,1,0:T(8,128)(2,1)S(1)}, u32[]{:S(2)}, u32[]{:S(2)}) collective-permute-start(bf16[2,128,128]{2,1,0:T(8,128)(2,1)S(1)} %add_convert_fusion.2), channel_id=1, source_target_pairs={{64,128},{65,129},{66,130},{67,131},{68,132},{69,133},{70,134},{71... | collective-permute-start | bytes 196616 | tf_op jit(solution)/shard_map/ppermute | solution.py:340
  184.5 5.4 %collective-permute-start.18 = (bf16[2,128,128]{2,1,0:T(8,128)(2,1)S(1)}, bf16[2,128,128]{2,1,0:T(8,128)(2,1)S(1)}, u32[]{:S(2)}, u32[]{:S(2)}) collective-permute-start(bf16[2,128,128]{2,1,0:T(8,128)(2,1)S(1)} %collective-permute-done.16.refs_0_.hidden_ref), channel_id=1, source_target_pairs={{0,32},{16,48},{32,0},{48,16},{1,33},{17,49},{33,1},{49,17},{2,34}... | collective-permute-start | bytes 196616 | tf_op jit(solution)/shard_map/ppermute | solution.py:89
  242.4 13.0 %collective-permute-start.24 = (bf16[2,128,128]{2,1,0:T(8,128)(2,1)S(1)}, bf16[2,128,128]{2,1,0:T(8,128)(2,1)S(1)}, u32[]{:S(2)}, u32[]{:S(2)}) collective-permute-start(bf16[2,128,128]{2,1,0:T(8,128)(2,1)S(1)} %collective-permute-done.23.refs_0_.hidden_ref), channel_id=1, source_target_pairs={{0,16},{16,32},{32,48},{48,0},{1,17},{17,33},{33,49},{49,1},{2,18}... | collective-permute-start | bytes 196616 | tf_op jit(solution)/shard_map/ppermute | solution.py:89
  251.5 5.2 %collective-permute-start.25 = (bf16[2,128,128]{2,1,0:T(8,128)(2,1)S(1)}, bf16[2,128,128]{2,1,0:T(8,128)(2,1)S(1)}, u32[]{:S(2)}, u32[]{:S(2)}) collective-permute-start(bf16[2,128,128]{2,1,0:T(8,128)(2,1)S(1)} %collective-permute-done.23.refs_0_.hidden_ref), channel_id=1, source_target_pairs={{0,32},{16,48},{32,0},{48,16},{1,33},{17,49},{33,1},{49,17},{2,34}... | collective-permute-start | bytes 196616 | tf_op jit(solution)/shard_map/ppermute | solution.py:89
  305.3 22.7 %collective-permute-start.27 = (bf16[2,128,128]{2,1,0:T(8,128)(2,1)S(1)}, bf16[2,128,128]{2,1,0:T(8,128)(2,1)S(1)}, u32[]{:S(2)}, u32[]{:S(2)}) collective-permute-start(bf16[2,128,128]{2,1,0:T(8,128)(2,1)S(1)} %get-tuple-element.57), channel_id=1, source_target_pairs={{0,16},{16,32},{32,48},{48,0},{1,17},{17,33},{33,49},{49,1},{2,18}... | collective-permute-start | bytes 196616 | tf_op jit(solution)/shard_map/ppermute | solution.py:89
  305.4 22.6 %collective-permute-start.28 = (bf16[2,128,128]{2,1,0:T(8,128)(2,1)S(1)}, bf16[2,128,128]{2,1,0:T(8,128)(2,1)S(1)}, u32[]{:S(2)}, u32[]{:S(2)}) collective-permute-start(bf16[2,128,128]{2,1,0:T(8,128)(2,1)S(1)} %get-tuple-element.58), channel_id=1, source_target_pairs={{0,32},{16,48},{32,0},{48,16},{1,33},{17,49},{33,1},{49,17},{2,34}... | collective-permute-start | bytes 196616 | tf_op jit(solution)/shard_map/ppermute | solution.py:89
  307.8 20.1 %collective-permute-start.29 = (bf16[2,128,128]{2,1,0:T(8,128)(2,1)S(1)}, bf16[2,128,128]{2,1,0:T(8,128)(2,1)S(1)}, u32[]{:S(2)}, u32[]{:S(2)}) collective-permute-start(bf16[2,128,128]{2,1,0:T(8,128)(2,1)S(1)} %get-tuple-element.59), channel_id=1, source_target_pairs={{0,48},{16,0},{32,16},{48,32},{1,49},{17,1},{33,17},{49,33},{2,50}... | collective-permute-start | bytes 196616 | tf_op jit(solution)/shard_map/ppermute | solution.py:89
  309.0 19.0 %collective-permute-start.31 = (bf16[128,128]{1,0:T(8,128)(2,1)S(1)}, bf16[128,128]{1,0:T(8,128)(2,1)S(1)}, u32[]{:S(2)}, u32[]{:S(2)}) collective-permute-start(bf16[128,128]{1,0:T(8,128)(2,1)S(1)} %copy-done.21), channel_id=1, source_target_pairs={{0,1},{1,0},{2,3},{3,2},{4,5},{5,4},{6,7},{7,6},{8,9},{9,8},{10,11... | collective-permute-start | bytes 98312 | tf_op jit(solution)/shard_map/ppermute | solution.py:93
  338.1 5.7 %collective-permute-start.36 = (f32[8,128]{1,0:T(8,128)S(1)}, f32[8,128]{1,0:T(8,128)S(1)}, u32[]{:S(2)}, u32[]{:S(2)}) collective-permute-start(f32[8,128]{1,0:T(8,128)S(1)} %add.183), channel_id=1, source_target_pairs={{0,4},{2,6},{4,0},{6,2},{8,12},{10,14},{12,8},{14,10},{1,5},{3,7},... | collective-permute-start | bytes 12296 | tf_op jit(solution)/shard_map/ppermute | solution.py:217
  338.1 6.4 %collective-permute-start.37 = (f32[8,128]{1,0:T(8,128)S(1)}, f32[8,128]{1,0:T(8,128)S(1)}, u32[]{:S(2)}, u32[]{:S(2)}) collective-permute-start(f32[8,128]{1,0:T(8,128)S(1)} %add.183), channel_id=1, source_target_pairs={{0,8},{2,10},{4,12},{6,14},{8,0},{10,2},{12,4},{14,6},{1,9},{3,11}... | collective-permute-start | bytes 12296 | tf_op jit(solution)/shard_map/ppermute | solution.py:217
  346.1 5.9 %collective-permute-start.41 = (f32[8,128]{1,0:T(8,128)S(1)}, f32[8,128]{1,0:T(8,128)S(1)}, u32[]{:S(2)}, u32[]{:S(2)}) collective-permute-start(f32[8,128]{1,0:T(8,128)S(1)} %add_add_fusion), channel_id=1, source_target_pairs={{192,128},{193,129},{194,130},{195,131},{196,132},{197,133},{198,1... | collective-permute-start | bytes 12296 | tf_op jit(solution)/shard_map/ppermute | solution.py:348
  352.0 9.6 %collective-permute-start.42 = (f32[8,128]{1,0:T(8,128)S(1)}, f32[8,128]{1,0:T(8,128)S(1)}, u32[]{:S(2)}, u32[]{:S(2)}) collective-permute-start(f32[8,128]{1,0:T(8,128)S(1)} %add_select_fusion), channel_id=1, source_target_pairs={{0,1},{1,0},{2,3},{3,2},{4,5},{5,4},{6,7},{7,6},{8,9},{9,8},{10,11... | collective-permute-start | bytes 12296 | tf_op jit(solution)/shard_map/ppermute | solution.py:93
  360.9 15.0 %collective-permute-start.30 = (bf16[128,128]{1,0:T(8,128)(2,1)S(1)}, bf16[128,128]{1,0:T(8,128)(2,1)S(1)}, u32[]{:S(2)}, u32[]{:S(2)}) collective-permute-start(bf16[128,128]{1,0:T(8,128)(2,1)S(1)} %get-tuple-element.71), channel_id=1, source_target_pairs={{0,1},{1,0},{2,3},{3,2},{4,5},{5,4},{6,7},{7,6},{8,9},{9,8},{10,11... | collective-permute-start | bytes 98312 | tf_op jit(solution)/shard_map/ppermute | solution.py:93
  (44 other events, 379.6 us)
where the time goes:
time: 382 us; the launch traced here: 377 us
  blocking collectives  122 us (32%)
  starting transfers between devices  95.8 us (25%)
  waiting for transfers between devices  84.6 us (22%)
  Pallas kernels  41.9 us (11%)
  local copies, waits for them, and re-layouts  24.3 us (6%)
  between operations  3.86 us (1%)
    all_to_all x3, blocking collectives, local(): received = lax.all_to_all(project(around), 'z', 0, 0, tiled=True)  69.1 us
    all_to_all x3, blocking collectives, local(): heads = lax.all_to_all(attend(received), 'z', 0, 0, tiled=True)  53.3 us
    ppermute x24, starting transfers between devices, shifted(): lax.ppermute(array, axis, [(i, (i + by) % count) for i in range(count)])  39.3 us
    ppermute x6, starting transfers between devices, swapped(): return lax.ppermute(array, 'core', [(0, 1), (1, 0)])  28.9 us
    all_to_all x1, waiting for transfers between devices, local(): received = lax.all_to_all(project(around), 'z', 0, 0, tiled=True)  28.8 us
    unnamed x46, local copies, waits for them, and re-layouts  22.5 us
    all_to_all x1, waiting for transfers between devices, local(): heads = lax.all_to_all(attend(received), 'z', 0, 0, tiled=True)  17.9 us
    ppermute x24, waiting for transfers between devices, shifted(): lax.ppermute(array, axis, [(i, (i + by) % count) for i in range(count)])  17.4 us
  transfers between devices with their start and end apart: 45, of which 30 were waited for; matrix products, arithmetic and copies ran while one was open for 1% of the time, Pallas kernels for 3%

commit v1 on v0

--- a/solution.py
+++ b/solution.py
@@ -71,10 +71,15 @@
     other_ref[...] = (w - shift).astype(jnp.bfloat16)
 
 
-def update_kernel(rate_ref, *refs):
+def update_kernel(entries, sums_ref, *refs):
+    rate = learn_rate * ((sums_ref[0] / entries - sums_ref[1] / entries) / (2.0 * perturb_scale))
     count = len(refs) // 3
     for w_ref, z_ref, out_ref in zip(refs[:count], refs[count : 2 * count], refs[2 * count :]):
-        out_ref[...] = (w_ref[...].astype(jnp.float32) - rate_ref[0] * z_ref[...]).astype(jnp.bfloat16)
+        out_ref[...] = (w_ref[...].astype(jnp.float32) - rate * z_ref[...]).astype(jnp.bfloat16)
+
+
+def in_hbm(array):
+    return pltpu.with_memory_space_constraint(array, pltpu.HBM)
 
 
 def by_rows(array, steps):
@@ -238,7 +243,18 @@
     def salt(code):
         return mix_bits(mix_bits(step_count[0] * 40503 + (4 * section + code) * 1000003) ^ noise_seed[0])
 
+    gain_noise = noise_of(jnp.arange(full, dtype=jnp.int32), salt(0))
+    gains = (norm_gains[0] + amount * gain_noise).reshape(NY, NZ, NC, width)
+    gains = lax.dynamic_index_in_dim(gains, z, 1, keepdims=False)
+    gains = jnp.where(core == 0, gains, gains[:, ::-1])
+    gains = gains.transpose(1, 0, 2)
+    gains = jnp.concatenate([gains, gains], axis=1)[:, ::-1]
+    gains = lax.dynamic_slice_in_dim(gains, NY - 1 - y, NY, 1)
+
     wq, wk, wo = w_query[0, 0], w_keyval[0, 0], w_output[0, 0]
+    ints = jnp.stack([salt(1), salt(2), block * width, y * query_cols, y * keyval_cols])
+    ints_out = jnp.stack([salt(3), y * query_cols, block * width])
+    gains, ints, ints_out, gain_noise = lax.optimization_barrier((gains, ints, ints_out, gain_noise))
     paired = jax.ShapeDtypeStruct((wq.shape[0], query_cols + keyval_cols), jnp.bfloat16)
     zq, zk, in_mine, in_other = pl.pallas_call(
         functools.partial(perturb_input_kernel, full, spread, NY),
@@ -246,16 +262,16 @@
         in_specs=[SMEM, SMEM, by_rows(wq, NY), by_rows(wk, NY)],
         out_specs=[by_rows(wq, NY), by_rows(wk, NY), by_rows(paired, NY), by_rows(paired, NY)],
         out_shape=[
-            jax.ShapeDtypeStruct(wq.shape, jnp.float32),
-            jax.ShapeDtypeStruct(wk.shape, jnp.float32),
+            pltpu.HBM(wq.shape, jnp.float32),
+            pltpu.HBM(wk.shape, jnp.float32),
             paired,
             paired,
         ],
         compiler_params=limit(14),
         cost_estimate=noise_cost(wq.size + wk.size),
     )(
-        jnp.stack([salt(1), salt(2), block * width, y * query_cols, y * keyval_cols]),
-        amount.reshape(1), wq, wk,
+        ints,
+        amount.reshape(1), in_hbm(wq), in_hbm(wk),
     )
     in_part = swapped(in_other)
     hidden = jnp.stack([inputs, swapped(inputs)])
@@ -267,24 +283,18 @@
         in_specs=[SMEM, SMEM, by_rows(wo, 8)],
         out_specs=[by_rows(wo, 8)] * 3,
         out_shape=[
-            jax.ShapeDtypeStruct(wo.shape, jnp.float32),
+            pltpu.HBM(wo.shape, jnp.float32),
             jax.ShapeDtypeStruct(wo.shape, jnp.bfloat16),
             jax.ShapeDtypeStruct(wo.shape, jnp.bfloat16),
         ],
         compiler_params=limit(14),
         cost_estimate=noise_cost(wo.size),
     )(
-        jnp.stack([salt(3), y * query_cols, block * width]),
-        amount.reshape(1), wo,
+        ints_out,
+        amount.reshape(1), in_hbm(wo),
     )
     o_part = swapped(o_other)
-    in_mine, o_mine = lax.optimization_barrier((in_mine, o_mine))
-
-    gain_noise = noise_of(jnp.arange(full, dtype=jnp.int32), salt(0))
-    gains = (norm_gains[0] + amount * gain_noise).reshape(NY, NZ, NC, width)
-    gains = lax.dynamic_index_in_dim(gains, z, 1, keepdims=False)
-    gains = jnp.where(core == 0, gains, gains[:, ::-1])
-    gains = jnp.take(gains.transpose(1, 0, 2), (y - jnp.arange(NY)) % NY, axis=1)
+    in_mine, in_part, o_mine, o_part = lax.optimization_barrier((in_mine, in_part, o_mine, o_part))
 
     cosine, sine = (jnp.asarray(t) for t in rope_tables(tokens))
     place = y.reshape(1)
@@ -356,13 +366,13 @@
     arrays = (wq, wk, wo)
     specs = [by_rows(w, 8) for w in arrays]
     new_query, new_keyval, new_output = pl.pallas_call(
-        update_kernel,
+        functools.partial(update_kernel, float(tokens * full)),
         grid=(8,),
         in_specs=[SMEM] + specs + specs,
         out_specs=specs,
-        out_shape=[jax.ShapeDtypeStruct(w.shape, jnp.bfloat16) for w in arrays],
+        out_shape=[pltpu.HBM(w.shape, jnp.bfloat16) for w in arrays],
         compiler_params=limit(14),
-    )(rate.reshape(1), *arrays, zq, zk, zo)
+    )(squared, *map(in_hbm, (*arrays, zq, zk, zo)))
     mine, other = record[0], swapped(record[1])
     layer_outputs = jnp.where(core == 0, jnp.stack([mine, other]), jnp.stack([other, mine]))[None]
     return (

time: 382 us -> 344 us (0.901); the launches traced: 377 us -> 343 us
  blocking collectives: 122 us -> 175 us
  waiting for transfers between devices: 84.6 us -> 45.1 us
  local copies, waits for them, and re-layouts: 24.3 us -> 2.06 us
  starting transfers between devices: 95.8 us -> 77.7 us
  Pallas kernels: 41.9 us -> 35.6 us
    all_to_all x2 -> x0, waiting for transfers between devices: 46.7 us -> none  [the longest x1 28.8 us: local(): received = lax.all_to_all(project(around), 'z', 0, 0, tiled=True)]
    all_to_all x3 -> x4, blocking collectives: 69.1 us -> 103 us  [local(): received = lax.all_to_all(project(around), 'z', 0, 0, tiled=True)]
    unnamed x46 -> x10, local copies, waits for them, and re-layouts: 22.5 us -> 0.03 us
    all_to_all x3 -> x4, blocking collectives: 53.3 us -> 72.5 us  [local(): heads = lax.all_to_all(attend(received), 'z', 0, 0, tiled=True)]
    all_to_all x2 -> x0, starting transfers between devices: 11.8 us -> none  [the longest x1 8.33 us: local(): received = lax.all_to_all(project(around), 'z', 0, 0, tiled=True)]
    ppermute x24, starting transfers between devices: 39.3 us -> 29.1 us  [shifted(): lax.ppermute(array, axis, [(i, (i + by) % count) for i in range(count)])]
    pallas_call x4, Pallas kernels: 10.6 us -> 3.63 us  [project(): pl.pallas_call(project_kernel, in_specs=[SMEM] + [VMEM] * (NY + 3), out_s...]
    pallas_call x4, Pallas kernels: 10 us -> 3.54 us  [output(): pl.pallas_call(output_kernel, in_specs=[SMEM] + [VMEM] * 4, out_specs=[VM...]
  transfers between devices with their start and end apart: 45 -> 43, of which waited for: 30 -> 31; matrix products, arithmetic and copies ran while one was open for 1% -> 1% of each run, Pallas kernels for 3% -> 5%
where the time goes in v1:
time: 344 us; the launch traced here: 343 us
  blocking collectives  175 us (51%)
  starting transfers between devices  77.7 us (23%)
  waiting for transfers between devices  45.1 us (13%)
  Pallas kernels  35.6 us (10%)
  between operations  3.68 us (1%)
  other arithmetic  3.49 us (1%)
    all_to_all x4, blocking collectives, local(): received = lax.all_to_all(project(around), 'z', 0, 0, tiled=True)  103 us
    all_to_all x4, blocking collectives, local(): heads = lax.all_to_all(attend(received), 'z', 0, 0, tiled=True)  72.5 us
    ppermute x6, starting transfers between devices, swapped(): return lax.ppermute(array, 'core', [(0, 1), (1, 0)])  32.8 us
    ppermute x24, starting transfers between devices, shifted(): lax.ppermute(array, axis, [(i, (i + by) % count) for i in range(count)])  29.1 us
    ppermute x24, waiting for transfers between devices, shifted(): lax.ppermute(array, axis, [(i, (i + by) % count) for i in range(count)])  21.5 us
    ppermute x7, starting transfers between devices, summed_over(): lax.ppermute(value, axis, [(i, i ^ step) for i in range(count)])  9.98 us
    pallas_call x1, Pallas kernels, local(): pl.pallas_call(functools.partial(update_kernel, float(tokens * full)), gr...  8.91 us
    pallas_call x1, Pallas kernels, local(): pl.pallas_call(functools.partial(perturb_output_kernel, full, spread, wid...  7.77 us
  transfers between devices with their start and end apart: 43, of which 31 were waited for; matrix products, arithmetic and copies ran while one was open for 1% of the time, Pallas kernels for 5%

profile of v1, /device:TPU:5, one launch (start us, length us, event | category | flops | bytes accessed | tf_op | source)
XLA Modules:
  0.0 342.6 jit_solution(14161673297292563219)
XLA Ops:
  3.1 7.2 %shard_map.145 = (f32[512,2048]{1,0:T(8,128)}, f32[512,512]{1,0:T(8,128)}, bf16[512,2560]{1,0:T(8,128)(2,1)S(1)}, bf16[512,2560]{1,0:T(8,128)(2,1)S(1)}) custom-call(s32[5]{0:T(128)S(1)} %stack.78.ints_ref, f32[1]{0:T(128)} %bitcast.15.sign_ref, bf16[512,2048]{1,0:T(8,128)(2,1)} %bitcast.41, bf16[512,512]{1,0:T(8,128)(2,1)} %bitcast.45), custom_call_target="tpu_custom_call" | custom-call | flops 78643200 | bytes 13107200 | tf_op jit(solution)/shard_map/pallas_call | solution.py:259
  11.0 4.5 %collective-permute-done = bf16[128,128]{1,0:T(8,128)(2,1)S(1)} collective-permute-done((bf16[128,128]{1,0:T(8,128)(2,1)S(1)}, bf16[128,128]{1,0:T(8,128)(2,1)S(1)}, u32[]{:S(2)}, u32[]{:S(2)}) %collective-permute-start) | collective-permute-done | bytes 32800 | tf_op jit(solution)/shard_map/ppermute | solution.py:98
  16.8 3.1 collective-permute-done.1.refs_1_
  19.9 7.8 %shard_map.146 = (f32[2048,512]{1,0:T(8,128)}, bf16[2048,512]{1,0:T(8,128)(2,1)S(1)}, bf16[2048,512]{1,0:T(8,128)(2,1)S(1)}) custom-call(s32[3]{0:T(128)S(1)} %pad_add_fusion.ints_ref, f32[1]{0:T(128)} %bitcast.15.sign_ref, bf16[2048,512]{1,0:T(8,128)(2,1)} %bitcast.43), custom_call_target="tpu_custom_call" | custom-call | flops 62914560 | bytes 10485760 | tf_op jit(solution)/shard_map/pallas_call | solution.py:280
  35.9 35.6 %all_to_all.40.recv_ref = bf16[8,528,128]{2,1,0:T(8,128)(2,1)S(1)} all-to-all(bf16[8,528,128]{2,1,0:T(8,128)(2,1)S(1)} %shard_map.147), channel_id=1, replica_groups=mesh['section'=4,'y'=4,'z'=8,'core'=2] {'z'}, dimensions={0} | all-to-all | bytes 2162688 | tf_op jit(solution)/shard_map/all_to_all | solution.py:342
  72.7 17.8 %all_to_all.41.heads_ref = bf16[8,256,128]{2,1,0:T(8,128)(2,1)S(1)} all-to-all(bf16[8,256,128]{2,1,0:T(8,128)(2,1)S(1)} %shard_map.148), channel_id=1, replica_groups=mesh['section'=4,'y'=4,'z'=8,'core'=2] {'z'}, dimensions={0} | all-to-all | bytes 1048576 | tf_op jit(solution)/shard_map/all_to_all | solution.py:343
  92.6 2.5 collective-permute-start.7
  105.6 26.0 %all_to_all.42.recv_ref = bf16[8,528,128]{2,1,0:T(8,128)(2,1)S(1)} all-to-all(bf16[8,528,128]{2,1,0:T(8,128)(2,1)S(1)} %shard_map.150), channel_id=1, replica_groups=mesh['section'=4,'y'=4,'z'=8,'core'=2] {'z'}, dimensions={0} | all-to-all | bytes 2162688 | tf_op jit(solution)/shard_map/all_to_all | solution.py:342
  132.7 16.0 %all_to_all.43.heads_ref = bf16[8,256,128]{2,1,0:T(8,128)(2,1)S(1)} all-to-all(bf16[8,256,128]{2,1,0:T(8,128)(2,1)S(1)} %shard_map.151), channel_id=1, replica_groups=mesh['section'=4,'y'=4,'z'=8,'core'=2] {'z'}, dimensions={0} | all-to-all | bytes 1048576 | tf_op jit(solution)/shard_map/all_to_all | solution.py:343
  151.0 2.4 collective-permute-start.14
  157.8 5.5 %collective-permute-done.16.refs_0_.hidden_ref = bf16[2,128,128]{2,1,0:T(8,128)(2,1)S(1)} collective-permute-done((bf16[2,128,128]{2,1,0:T(8,128)(2,1)S(1)}, bf16[2,128,128]{2,1,0:T(8,128)(2,1)S(1)}, u32[]{:S(2)}, u32[]{:S(2)}) %collective-permute-start.16) | collective-permute-done | bytes 65568 | tf_op jit(solution)/shard_map/ppermute | solution.py:350
  163.3 2.8 collective-permute-start.18
  170.1 20.5 %all_to_all.44.recv_ref = bf16[8,528,128]{2,1,0:T(8,128)(2,1)S(1)} all-to-all(bf16[8,528,128]{2,1,0:T(8,128)(2,1)S(1)} %shard_map.153), channel_id=1, replica_groups=mesh['section'=4,'y'=4,'z'=8,'core'=2] {'z'}, dimensions={0} | all-to-all | bytes 2162688 | tf_op jit(solution)/shard_map/all_to_all | solution.py:342
  191.7 18.2 %all_to_all.45.heads_ref = bf16[8,256,128]{2,1,0:T(8,128)(2,1)S(1)} all-to-all(bf16[8,256,128]{2,1,0:T(8,128)(2,1)S(1)} %shard_map.154), channel_id=1, replica_groups=mesh['section'=4,'y'=4,'z'=8,'core'=2] {'z'}, dimensions={0} | all-to-all | bytes 1048576 | tf_op jit(solution)/shard_map/all_to_all | solution.py:343
  210.9 2.5 collective-permute-start.21
  220.2 2.8 collective-permute-start.25
  227.1 20.5 %all_to_all.46.recv_ref = bf16[8,528,128]{2,1,0:T(8,128)(2,1)S(1)} all-to-all(bf16[8,528,128]{2,1,0:T(8,128)(2,1)S(1)} %shard_map.156), channel_id=1, replica_groups=mesh['section'=4,'y'=4,'z'=8,'core'=2] {'z'}, dimensions={0} | all-to-all | bytes 2162688 | tf_op jit(solution)/shard_map/all_to_all | solution.py:342
  248.7 20.5 %all_to_all.47.heads_ref = bf16[8,256,128]{2,1,0:T(8,128)(2,1)S(1)} all-to-all(bf16[8,256,128]{2,1,0:T(8,128)(2,1)S(1)} %shard_map.157), channel_id=1, replica_groups=mesh['section'=4,'y'=4,'z'=8,'core'=2] {'z'}, dimensions={0} | all-to-all | bytes 1048576 | tf_op jit(solution)/shard_map/all_to_all | solution.py:343
  270.2 2.5 collective-permute-start.28
  273.8 21.6 %collective-permute-start.31 = (bf16[128,128]{1,0:T(8,128)(2,1)S(1)}, bf16[128,128]{1,0:T(8,128)(2,1)S(1)}, u32[]{:S(2)}, u32[]{:S(2)}) collective-permute-start(bf16[128,128]{1,0:T(8,128)(2,1)S(1)} %copy-done.3), channel_id=1, source_target_pairs={{0,1},{1,0},{2,3},{3,2},{4,5},{5,4},{6,7},{7,6},{8,9},{9,8},{10,11... | collective-permute-start | bytes 98312 | tf_op jit(solution)/shard_map/ppermute | solution.py:98
  308.4 3.6 %collective-permute-start.38 = (f32[8,128]{1,0:T(8,128)S(1)}, f32[8,128]{1,0:T(8,128)S(1)}, u32[]{:S(2)}, u32[]{:S(2)}) collective-permute-start(f32[8,128]{1,0:T(8,128)S(1)} %add.139), channel_id=1, source_target_pairs={{0,12},{2,14},{4,8},{6,10},{8,4},{10,6},{12,0},{14,2},{1,13},{3,15... | collective-permute-start | bytes 12296 | tf_op jit(solution)/shard_map/ppermute | solution.py:222
  315.7 4.5 %collective-permute-done.41 = f32[8,128]{1,0:T(8,128)S(1)} collective-permute-done((f32[8,128]{1,0:T(8,128)S(1)}, f32[8,128]{1,0:T(8,128)S(1)}, u32[]{:S(2)}, u32[]{:S(2)}) %collective-permute-start.41) | collective-permute-done | bytes 4128 | tf_op jit(solution)/shard_map/ppermute | solution.py:358
  320.3 8.8 %collective-permute-start.42 = (f32[8,128]{1,0:T(8,128)S(1)}, f32[8,128]{1,0:T(8,128)S(1)}, u32[]{:S(2)}, u32[]{:S(2)}) collective-permute-start(f32[8,128]{1,0:T(8,128)S(1)} %add_select_fusion), channel_id=1, source_target_pairs={{0,1},{1,0},{2,3},{3,2},{4,5},{5,4},{6,7},{7,6},{8,9},{9,8},{10,11... | collective-permute-start | bytes 12296 | tf_op jit(solution)/shard_map/ppermute | solution.py:98
  333.1 8.9 %shard_map.159 = (bf16[512,2048]{1,0:T(8,128)(2,1)}, bf16[512,512]{1,0:T(8,128)(2,1)}, bf16[2048,512]{1,0:T(8,128)(2,1)}) custom-call(f32[2]{0:T(128)S(1)} %get-tuple-element.78.sums_ref, bf16[512,2048]{1,0:T(8,128)(2,1)} %bitcast.42, bf16[512,512]{1,0:T(8,128)(2,1)} %bitcast.46, bf16[2048,512]{1,0:T(8,128)(2,1)} %bitcast.44, ...), custom_call_target="tpu_custom_call" | custom-call | tf_op jit(solution)/shard_map/pallas_call | solution.py:368
  (123 shorter events, 73.0 us)
Async XLA Ops:
  10.2 22.8 %collective-permute-start.4 = (bf16[512,2560]{1,0:T(8,128)(2,1)S(1)}, bf16[512,2560]{1,0:T(8,128)(2,1)S(1)}, u32[]{:S(2)}, u32[]{:S(2)}) collective-permute-start(bf16[512,2560]{1,0:T(8,128)(2,1)S(1)} %get-tuple-element.46), channel_id=1, source_target_pairs={{0,1},{1,0},{2,3},{3,2},{4,5},{5,4},{6,7},{7,6},{8,9},{9,8},{10,11... | collective-permute-start | bytes 7864328 | tf_op jit(solution)/shard_map/ppermute | solution.py:98
  10.9 4.6 %collective-permute-start = (bf16[128,128]{1,0:T(8,128)(2,1)S(1)}, bf16[128,128]{1,0:T(8,128)(2,1)S(1)}, u32[]{:S(2)}, u32[]{:S(2)}) collective-permute-start(bf16[128,128]{1,0:T(8,128)(2,1)S(1)} %copy-done.4), channel_id=1, source_target_pairs={{0,1},{1,0},{2,3},{3,2},{4,5},{5,4},{6,7},{7,6},{8,9},{9,8},{10,11... | collective-permute-start | bytes 98312 | tf_op jit(solution)/shard_map/ppermute | solution.py:98
  27.7 5.3 %collective-permute-start.5 = (bf16[2048,512]{1,0:T(8,128)(2,1)S(1)}, bf16[2048,512]{1,0:T(8,128)(2,1)S(1)}, u32[]{:S(2)}, u32[]{:S(2)}) collective-permute-start(bf16[2048,512]{1,0:T(8,128)(2,1)S(1)} %get-tuple-element.50), channel_id=1, source_target_pairs={{0,1},{1,0},{2,3},{3,2},{4,5},{5,4},{6,7},{7,6},{8,9},{9,8},{10,11... | collective-permute-start | bytes 6291464 | tf_op jit(solution)/shard_map/ppermute | solution.py:98
  29.2 5.2 %collective-permute-start.2 = (bf16[2,128,128]{2,1,0:T(8,128)(2,1)S(1)}, bf16[2,128,128]{2,1,0:T(8,128)(2,1)S(1)}, u32[]{:S(2)}, u32[]{:S(2)}) collective-permute-start(bf16[2,128,128]{2,1,0:T(8,128)(2,1)S(1)} %pad_maximum_fusion.refs_0_.hidden_ref), channel_id=1, source_target_pairs={{0,32},{16,48},{32,0},{48,16},{1,33},{17,49},{33,1},{49,17},{2,34}... | collective-permute-start | bytes 196616 | tf_op jit(solution)/shard_map/ppermute | solution.py:94
  92.6 4.9 %collective-permute-start.7 = (bf16[2,128,128]{2,1,0:T(8,128)(2,1)S(1)}, bf16[2,128,128]{2,1,0:T(8,128)(2,1)S(1)}, u32[]{:S(2)}, u32[]{:S(2)}) collective-permute-start(bf16[2,128,128]{2,1,0:T(8,128)(2,1)S(1)} %get-tuple-element.57), channel_id=1, source_target_pairs={{0,32},{16,48},{32,0},{48,16},{1,33},{17,49},{33,1},{49,17},{2,34}... | collective-permute-start | bytes 196616 | tf_op jit(solution)/shard_map/ppermute | solution.py:94
  99.0 5.1 %collective-permute-start.10 = (bf16[2,128,128]{2,1,0:T(8,128)(2,1)S(1)}, bf16[2,128,128]{2,1,0:T(8,128)(2,1)S(1)}, u32[]{:S(2)}, u32[]{:S(2)}) collective-permute-start(bf16[2,128,128]{2,1,0:T(8,128)(2,1)S(1)} %collective-permute-done.9.refs_0_.hidden_ref), channel_id=1, source_target_pairs={{0,16},{16,32},{32,48},{48,0},{1,17},{17,33},{33,49},{49,1},{2,18}... | collective-permute-start | bytes 196616 | tf_op jit(solution)/shard_map/ppermute | solution.py:94
  99.1 5.0 %collective-permute-start.11 = (bf16[2,128,128]{2,1,0:T(8,128)(2,1)S(1)}, bf16[2,128,128]{2,1,0:T(8,128)(2,1)S(1)}, u32[]{:S(2)}, u32[]{:S(2)}) collective-permute-start(bf16[2,128,128]{2,1,0:T(8,128)(2,1)S(1)} %collective-permute-done.9.refs_0_.hidden_ref), channel_id=1, source_target_pairs={{0,32},{16,48},{32,0},{48,16},{1,33},{17,49},{33,1},{49,17},{2,34}... | collective-permute-start | bytes 196616 | tf_op jit(solution)/shard_map/ppermute | solution.py:94
  151.0 4.9 %collective-permute-start.14 = (bf16[2,128,128]{2,1,0:T(8,128)(2,1)S(1)}, bf16[2,128,128]{2,1,0:T(8,128)(2,1)S(1)}, u32[]{:S(2)}, u32[]{:S(2)}) collective-permute-start(bf16[2,128,128]{2,1,0:T(8,128)(2,1)S(1)} %get-tuple-element.61), channel_id=1, source_target_pairs={{0,32},{16,48},{32,0},{48,16},{1,33},{17,49},{33,1},{49,17},{2,34}... | collective-permute-start | bytes 196616 | tf_op jit(solution)/shard_map/ppermute | solution.py:94
  156.5 6.8 %collective-permute-start.16 = (bf16[2,128,128]{2,1,0:T(8,128)(2,1)S(1)}, bf16[2,128,128]{2,1,0:T(8,128)(2,1)S(1)}, u32[]{:S(2)}, u32[]{:S(2)}) collective-permute-start(bf16[2,128,128]{2,1,0:T(8,128)(2,1)S(1)} %add_convert_fusion.2), channel_id=1, source_target_pairs={{64,128},{65,129},{66,130},{67,131},{68,132},{69,133},{70,134},{71... | collective-permute-start | bytes 196616 | tf_op jit(solution)/shard_map/ppermute | solution.py:350
  163.3 5.1 %collective-permute-start.18 = (bf16[2,128,128]{2,1,0:T(8,128)(2,1)S(1)}, bf16[2,128,128]{2,1,0:T(8,128)(2,1)S(1)}, u32[]{:S(2)}, u32[]{:S(2)}) collective-permute-start(bf16[2,128,128]{2,1,0:T(8,128)(2,1)S(1)} %collective-permute-done.16.refs_0_.hidden_ref), channel_id=1, source_target_pairs={{0,32},{16,48},{32,0},{48,16},{1,33},{17,49},{33,1},{49,17},{2,34}... | collective-permute-start | bytes 196616 | tf_op jit(solution)/shard_map/ppermute | solution.py:94
  210.8 5.1 %collective-permute-start.20 = (bf16[2,128,128]{2,1,0:T(8,128)(2,1)S(1)}, bf16[2,128,128]{2,1,0:T(8,128)(2,1)S(1)}, u32[]{:S(2)}, u32[]{:S(2)}) collective-permute-start(bf16[2,128,128]{2,1,0:T(8,128)(2,1)S(1)} %get-tuple-element.64), channel_id=1, source_target_pairs={{0,16},{16,32},{32,48},{48,0},{1,17},{17,33},{33,49},{49,1},{2,18}... | collective-permute-start | bytes 196616 | tf_op jit(solution)/shard_map/ppermute | solution.py:94
  210.9 5.0 %collective-permute-start.21 = (bf16[2,128,128]{2,1,0:T(8,128)(2,1)S(1)}, bf16[2,128,128]{2,1,0:T(8,128)(2,1)S(1)}, u32[]{:S(2)}, u32[]{:S(2)}) collective-permute-start(bf16[2,128,128]{2,1,0:T(8,128)(2,1)S(1)} %get-tuple-element.65), channel_id=1, source_target_pairs={{0,32},{16,48},{32,0},{48,16},{1,33},{17,49},{33,1},{49,17},{2,34}... | collective-permute-start | bytes 196616 | tf_op jit(solution)/shard_map/ppermute | solution.py:94
  219.5 4.6 %collective-permute-start.24 = (bf16[2,128,128]{2,1,0:T(8,128)(2,1)S(1)}, bf16[2,128,128]{2,1,0:T(8,128)(2,1)S(1)}, u32[]{:S(2)}, u32[]{:S(2)}) collective-permute-start(bf16[2,128,128]{2,1,0:T(8,128)(2,1)S(1)} %collective-permute-done.23.refs_0_.hidden_ref), channel_id=1, source_target_pairs={{0,16},{16,32},{32,48},{48,0},{1,17},{17,33},{33,49},{49,1},{2,18}... | collective-permute-start | bytes 196616 | tf_op jit(solution)/shard_map/ppermute | solution.py:94
  220.2 5.2 %collective-permute-start.25 = (bf16[2,128,128]{2,1,0:T(8,128)(2,1)S(1)}, bf16[2,128,128]{2,1,0:T(8,128)(2,1)S(1)}, u32[]{:S(2)}, u32[]{:S(2)}) collective-permute-start(bf16[2,128,128]{2,1,0:T(8,128)(2,1)S(1)} %collective-permute-done.23.refs_0_.hidden_ref), channel_id=1, source_target_pairs={{0,32},{16,48},{32,0},{48,16},{1,33},{17,49},{33,1},{49,17},{2,34}... | collective-permute-start | bytes 196616 | tf_op jit(solution)/shard_map/ppermute | solution.py:94
  270.1 26.1 %collective-permute-start.27 = (bf16[2,128,128]{2,1,0:T(8,128)(2,1)S(1)}, bf16[2,128,128]{2,1,0:T(8,128)(2,1)S(1)}, u32[]{:S(2)}, u32[]{:S(2)}) collective-permute-start(bf16[2,128,128]{2,1,0:T(8,128)(2,1)S(1)} %get-tuple-element.68), channel_id=1, source_target_pairs={{0,16},{16,32},{32,48},{48,0},{1,17},{17,33},{33,49},{49,1},{2,18}... | collective-permute-start | bytes 196616 | tf_op jit(solution)/shard_map/ppermute | solution.py:94
  270.2 26.0 %collective-permute-start.28 = (bf16[2,128,128]{2,1,0:T(8,128)(2,1)S(1)}, bf16[2,128,128]{2,1,0:T(8,128)(2,1)S(1)}, u32[]{:S(2)}, u32[]{:S(2)}) collective-permute-start(bf16[2,128,128]{2,1,0:T(8,128)(2,1)S(1)} %get-tuple-element.69), channel_id=1, source_target_pairs={{0,32},{16,48},{32,0},{48,16},{1,33},{17,49},{33,1},{49,17},{2,34}... | collective-permute-start | bytes 196616 | tf_op jit(solution)/shard_map/ppermute | solution.py:94
  272.7 23.6 %collective-permute-start.29 = (bf16[2,128,128]{2,1,0:T(8,128)(2,1)S(1)}, bf16[2,128,128]{2,1,0:T(8,128)(2,1)S(1)}, u32[]{:S(2)}, u32[]{:S(2)}) collective-permute-start(bf16[2,128,128]{2,1,0:T(8,128)(2,1)S(1)} %get-tuple-element.70), channel_id=1, source_target_pairs={{0,48},{16,0},{32,16},{48,32},{1,49},{17,1},{33,17},{49,33},{2,50}... | collective-permute-start | bytes 196616 | tf_op jit(solution)/shard_map/ppermute | solution.py:94
  273.8 22.5 %collective-permute-start.31 = (bf16[128,128]{1,0:T(8,128)(2,1)S(1)}, bf16[128,128]{1,0:T(8,128)(2,1)S(1)}, u32[]{:S(2)}, u32[]{:S(2)}) collective-permute-start(bf16[128,128]{1,0:T(8,128)(2,1)S(1)} %copy-done.3), channel_id=1, source_target_pairs={{0,1},{1,0},{2,3},{3,2},{4,5},{5,4},{6,7},{7,6},{8,9},{9,8},{10,11... | collective-permute-start | bytes 98312 | tf_op jit(solution)/shard_map/ppermute | solution.py:98
  306.4 5.7 %collective-permute-start.36 = (f32[8,128]{1,0:T(8,128)S(1)}, f32[8,128]{1,0:T(8,128)S(1)}, u32[]{:S(2)}, u32[]{:S(2)}) collective-permute-start(f32[8,128]{1,0:T(8,128)S(1)} %add.139), channel_id=1, source_target_pairs={{0,4},{2,6},{4,0},{6,2},{8,12},{10,14},{12,8},{14,10},{1,5},{3,7},... | collective-permute-start | bytes 12296 | tf_op jit(solution)/shard_map/ppermute | solution.py:222
  306.4 6.4 %collective-permute-start.37 = (f32[8,128]{1,0:T(8,128)S(1)}, f32[8,128]{1,0:T(8,128)S(1)}, u32[]{:S(2)}, u32[]{:S(2)}) collective-permute-start(f32[8,128]{1,0:T(8,128)S(1)} %add.139), channel_id=1, source_target_pairs={{0,8},{2,10},{4,12},{6,14},{8,0},{10,2},{12,4},{14,6},{1,9},{3,11}... | collective-permute-start | bytes 12296 | tf_op jit(solution)/shard_map/ppermute | solution.py:222
  308.4 4.6 %collective-permute-start.38 = (f32[8,128]{1,0:T(8,128)S(1)}, f32[8,128]{1,0:T(8,128)S(1)}, u32[]{:S(2)}, u32[]{:S(2)}) collective-permute-start(f32[8,128]{1,0:T(8,128)S(1)} %add.139), channel_id=1, source_target_pairs={{0,12},{2,14},{4,8},{6,10},{8,4},{10,6},{12,0},{14,2},{1,13},{3,15... | collective-permute-start | bytes 12296 | tf_op jit(solution)/shard_map/ppermute | solution.py:222
  314.4 5.9 %collective-permute-start.41 = (f32[8,128]{1,0:T(8,128)S(1)}, f32[8,128]{1,0:T(8,128)S(1)}, u32[]{:S(2)}, u32[]{:S(2)}) collective-permute-start(f32[8,128]{1,0:T(8,128)S(1)} %add_add_fusion), channel_id=1, source_target_pairs={{192,128},{193,129},{194,130},{195,131},{196,132},{197,133},{198,1... | collective-permute-start | bytes 12296 | tf_op jit(solution)/shard_map/ppermute | solution.py:358
  320.3 9.6 %collective-permute-start.42 = (f32[8,128]{1,0:T(8,128)S(1)}, f32[8,128]{1,0:T(8,128)S(1)}, u32[]{:S(2)}, u32[]{:S(2)}) collective-permute-start(f32[8,128]{1,0:T(8,128)S(1)} %add_select_fusion), channel_id=1, source_target_pairs={{0,1},{1,0},{2,3},{3,2},{4,5},{5,4},{6,7},{7,6},{8,9},{9,8},{10,11... | collective-permute-start | bytes 12296 | tf_op jit(solution)/shard_map/ppermute | solution.py:98
  329.1 12.9 %collective-permute-start.30 = (bf16[128,128]{1,0:T(8,128)(2,1)S(1)}, bf16[128,128]{1,0:T(8,128)(2,1)S(1)}, u32[]{:S(2)}, u32[]{:S(2)}) collective-permute-start(bf16[128,128]{1,0:T(8,128)(2,1)S(1)} %get-tuple-element.83), channel_id=1, source_target_pairs={{0,1},{1,0},{2,3},{3,2},{4,5},{5,4},{6,7},{7,6},{8,9},{9,8},{10,11... | collective-permute-start | bytes 98312 | tf_op jit(solution)/shard_map/ppermute | solution.py:98
  (24 other events, 212.1 us)

commit v2 on v1

--- a/solution.py
+++ b/solution.py
@@ -32,8 +32,7 @@
 
 def noise_of(index, salt):
     hashed = mix_bits(mix_bits(index ^ salt) + salt)
-    uniform_part = logical(hashed, 8).astype(jnp.float32) * (1.0 / 16777216.0)
-    return (uniform_part - 0.5) * 3.4641016
+    return logical(hashed, 8).astype(jnp.float32) * (3.4641016 / 16777216.0) - 0.5 * 3.4641016
 
 
 def limit(mib):
@@ -51,7 +50,7 @@
         width = w_ref.shape[1]
         col = lax.broadcasted_iota(jnp.int32, (1, width), 1) + first
         z = noise_of(row * cols + col, salt)
-        z_ref[...] = z
+        z_ref[...] = z.astype(jnp.bfloat16)
         w = w_ref[...].astype(jnp.float32)
         shift = sign_ref[0] * z
         mine_ref[:, at : at + width] = (w + shift).astype(jnp.bfloat16)
@@ -64,18 +63,49 @@
     col = lax.broadcasted_iota(jnp.int32, (1, cols), 1)
     col = col + col // width * (spread - width) + ints_ref[2]
     z = noise_of(row * full + col, ints_ref[0])
-    z_ref[...] = z
+    z_ref[...] = z.astype(jnp.bfloat16)
     w = w_ref[...].astype(jnp.float32)
     shift = sign_ref[0] * z
     mine_ref[...] = (w + shift).astype(jnp.bfloat16)
     other_ref[...] = (w - shift).astype(jnp.bfloat16)
 
 
-def update_kernel(entries, sums_ref, *refs):
-    rate = learn_rate * ((sums_ref[0] / entries - sums_ref[1] / entries) / (2.0 * perturb_scale))
+def finish_kernel(base_ref, *refs):
+    pieces = refs[: NY - 1]
+    goal_ref, result_ref, gap_ref = refs[NY - 1 :]
+    total = jnp.zeros(gap_ref.shape, jnp.float32)
+    for half in range(NC):
+        summed = base_ref[half]
+        for piece in pieces:
+            summed = summed + piece[half].astype(jnp.float32)
+        result = summed.astype(jnp.bfloat16)
+        result_ref[half] = result
+        gap = result.astype(jnp.float32) - goal_ref[half].astype(jnp.float32)
+        total = total + jnp.sum((gap * gap).reshape((-1,) + gap_ref.shape), axis=0)
+    gap_ref[...] = total
+
+
+def update_kernel(entries, core_ref, own_ref, partner_ref, gain_ref, noise_ref, *refs):
+    rate_ref = refs[-1]
+    loss_ref, new_gain_ref = refs[-3], refs[-2]
+    refs = refs[:-3]
+
+    @pl.when(pl.program_id(0) == 0)
+    def _():
+        own = jnp.sum(own_ref[...]) / entries
+        partner = jnp.sum(partner_ref[...]) / entries
+        first = core_ref[0] == 0
+        plus = jnp.where(first, own, partner)
+        minus = jnp.where(first, partner, own)
+        loss_ref[0, 0] = plus
+        loss_ref[0, 1] = minus
+        rate_ref[0] = learn_rate * ((plus - minus) / (2.0 * perturb_scale))
+        new_gain_ref[...] = gain_ref[...] - rate_ref[0] * noise_ref[...]
+
+    rate = rate_ref[0]
     count = len(refs) // 3
     for w_ref, z_ref, out_ref in zip(refs[:count], refs[count : 2 * count], refs[2 * count :]):
-        out_ref[...] = (w_ref[...].astype(jnp.float32) - rate * z_ref[...]).astype(jnp.bfloat16)
+        out_ref[...] = (w_ref[...].astype(jnp.float32) - rate * z_ref[...].astype(jnp.float32)).astype(jnp.bfloat16)
 
 
 def in_hbm(array):
@@ -254,7 +284,11 @@
     wq, wk, wo = w_query[0, 0], w_keyval[0, 0], w_output[0, 0]
     ints = jnp.stack([salt(1), salt(2), block * width, y * query_cols, y * keyval_cols])
     ints_out = jnp.stack([salt(3), y * query_cols, block * width])
-    gains, ints, ints_out, gain_noise = lax.optimization_barrier((gains, ints, ints_out, gain_noise))
+    hidden = jnp.stack([inputs, swapped(inputs)])
+    goal = jnp.stack([target, swapped(target)])
+    gains, ints, ints_out, gain_noise, hidden, goal = lax.optimization_barrier(
+        (gains, ints, ints_out, gain_noise, hidden, goal)
+    )
     paired = jax.ShapeDtypeStruct((wq.shape[0], query_cols + keyval_cols), jnp.bfloat16)
     zq, zk, in_mine, in_other = pl.pallas_call(
         functools.partial(perturb_input_kernel, full, spread, NY),
@@ -262,8 +296,8 @@
         in_specs=[SMEM, SMEM, by_rows(wq, NY), by_rows(wk, NY)],
         out_specs=[by_rows(wq, NY), by_rows(wk, NY), by_rows(paired, NY), by_rows(paired, NY)],
         out_shape=[
-            pltpu.HBM(wq.shape, jnp.float32),
-            pltpu.HBM(wk.shape, jnp.float32),
+            pltpu.HBM(wq.shape, jnp.bfloat16),
+            pltpu.HBM(wk.shape, jnp.bfloat16),
             paired,
             paired,
         ],
@@ -274,16 +308,14 @@
         amount.reshape(1), in_hbm(wq), in_hbm(wk),
     )
     in_part = swapped(in_other)
-    hidden = jnp.stack([inputs, swapped(inputs)])
     around = [hidden] + [shifted(hidden, "y", NY, k) for k in range(1, NY)]
-    wo, around[1] = lax.optimization_barrier((wo, around[1]))
     zo, o_mine, o_other = pl.pallas_call(
         functools.partial(perturb_output_kernel, full, spread, width),
-        grid=(8,),
-        in_specs=[SMEM, SMEM, by_rows(wo, 8)],
-        out_specs=[by_rows(wo, 8)] * 3,
+        grid=(4,),
+        in_specs=[SMEM, SMEM, by_rows(wo, 4)],
+        out_specs=[by_rows(wo, 4)] * 3,
         out_shape=[
-            pltpu.HBM(wo.shape, jnp.float32),
+            pltpu.HBM(wo.shape, jnp.bfloat16),
             jax.ShapeDtypeStruct(wo.shape, jnp.bfloat16),
             jax.ShapeDtypeStruct(wo.shape, jnp.bfloat16),
         ],
@@ -334,7 +366,6 @@
             compiler_params=limit(14),
         )(place, heads, o_mine, o_part, hidden)
 
-    goal = jnp.stack([target, swapped(target)])
     record = jnp.zeros_like(hidden)
     for tick in range(4):
         if tick:
@@ -342,42 +373,53 @@
         received = lax.all_to_all(project(around), "z", 0, 0, tiled=True)
         heads = lax.all_to_all(attend(received), "z", 0, 0, tiled=True)
         base, *pieces = output(heads, hidden)
-        for k in range(1, NY):
-            base = base + shifted(pieces[k - 1], "y", NY, k).astype(jnp.float32)
-        result = base.astype(jnp.bfloat16)
-        record = jnp.where(section == tick, result, record)
+        pieces = [shifted(piece, "y", NY, k) for k, piece in enumerate(pieces, 1)]
         if tick < 3:
+            for piece in pieces:
+                base = base + piece.astype(jnp.float32)
+            result = base.astype(jnp.bfloat16)
+            record = jnp.where(section == tick, result, record)
             hidden = lax.ppermute(result, "section", [(tick, tick + 1)])
-
-    gap = result.astype(jnp.float32) - goal.astype(jnp.float32)
-    squared = jnp.sum(gap * gap)
-    squared = jnp.full((8, LANE), squared)
+        else:
+            result, squared = pl.pallas_call(
+                finish_kernel,
+                in_specs=[VMEM] * (NY + 1),
+                out_specs=[VMEM] * 2,
+                out_shape=[
+                    jax.ShapeDtypeStruct(hidden.shape, jnp.bfloat16),
+                    jax.ShapeDtypeStruct((8, LANE), jnp.float32),
+                ],
+                compiler_params=limit(8),
+            )(base, *pieces, goal)
+            record = jnp.where(section == tick, result, record)
+
     squared = summed_over(squared, "y", (1, 2, 3))
     squared = summed_over(squared, "z", (1,))
     squared = summed_over(squared, "z", (2, 4, 6))
     copies = [lax.ppermute(squared, "section", [(sections - 1, k)]) for k in range(sections - 1)]
     squared = jnp.where(section == sections - 1, squared, sum(copies[1:], copies[0]))
+    mine, other = record[0], swapped(record[1])
+    layer_outputs = jnp.where(core == 0, jnp.stack([mine, other]), jnp.stack([other, mine]))[None]
+    squared, layer_outputs = lax.optimization_barrier((squared, layer_outputs))
     partner = swapped(squared)
-    squared = jnp.where(core == 0, jnp.stack([squared, partner]), jnp.stack([partner, squared]))[:, 0, 0]
-    losses = squared / (tokens * full)
-    rate = learn_rate * ((losses[0] - losses[1]) / (2.0 * perturb_scale))
-    new_gains = (norm_gains[0] - rate * gain_noise)[None]
 
     arrays = (wq, wk, wo)
     specs = [by_rows(w, 8) for w in arrays]
-    new_query, new_keyval, new_output = pl.pallas_call(
+    tile = pl.BlockSpec((8, LANE), lambda i: (0, 0))
+    line = pl.BlockSpec((1, full), lambda i: (0, 0))
+    new_query, new_keyval, new_output, losses, new_gains = pl.pallas_call(
         functools.partial(update_kernel, float(tokens * full)),
         grid=(8,),
-        in_specs=[SMEM] + specs + specs,
-        out_specs=specs,
-        out_shape=[pltpu.HBM(w.shape, jnp.bfloat16) for w in arrays],
+        in_specs=[SMEM, tile, tile, line, line] + specs + specs,
+        out_specs=specs + [SMEM, line],
+        out_shape=[pltpu.HBM(w.shape, jnp.bfloat16) for w in arrays]
+        + [jax.ShapeDtypeStruct((1, 2), jnp.float32), jax.ShapeDtypeStruct((1, full), jnp.float32)],
+        scratch_shapes=[pltpu.SMEM((1,), jnp.float32)],
         compiler_params=limit(14),
-    )(squared, *map(in_hbm, (*arrays, zq, zk, zo)))
-    mine, other = record[0], swapped(record[1])
-    layer_outputs = jnp.where(core == 0, jnp.stack([mine, other]), jnp.stack([other, mine]))[None]
+    )(core.reshape(1), squared, partner, norm_gains, gain_noise[None], *map(in_hbm, (*arrays, zq, zk, zo)))
     return (
         layer_outputs,
-        losses[None],
+        losses,
         new_gains,
         new_query[None, None],
         new_keyval[None, None],

time: 344 us -> 339 us (0.985); the launches traced: 343 us -> 334 us
  starting transfers between devices: 77.7 us -> 88.1 us
  waiting for transfers between devices: 45.1 us -> 35.7 us
    ppermute x24, starting transfers between devices: 29.1 us -> 39.1 us  [shifted(): lax.ppermute(array, axis, [(i, (i + by) % count) for i in range(count)])]
    ppermute x6, waiting for transfers between devices: 7.38 us -> 1.67 us  [swapped(): return lax.ppermute(array, 'core', [(0, 1), (1, 0)])]
    ppermute x3, waiting for transfers between devices: 4.55 us -> 0.01 us  [local(): lax.ppermute(squared, 'section', [(sections - 1, k)])]
  transfers between devices with their start and end apart: 43 -> 43, of which waited for: 31 -> 28; matrix products, arithmetic and copies ran while one was open for 1% -> 1% of each run, Pallas kernels for 5% -> 2%
where the time goes in v2:
time: 339 us; the launch traced here: 334 us
  blocking collectives  172 us (51%)
  starting transfers between devices  88.1 us (26%)
  waiting for transfers between devices  35.7 us (11%)
  Pallas kernels  32.8 us (10%)
    all_to_all x4, blocking collectives, local(): received = lax.all_to_all(project(around), 'z', 0, 0, tiled=True)  99.6 us
    all_to_all x4, blocking collectives, local(): heads = lax.all_to_all(attend(received), 'z', 0, 0, tiled=True)  72.1 us
    ppermute x24, starting transfers between devices, shifted(): lax.ppermute(array, axis, [(i, (i + by) % count) for i in range(count)])  39.1 us
    ppermute x6, starting transfers between devices, swapped(): return lax.ppermute(array, 'core', [(0, 1), (1, 0)])  32.6 us
    ppermute x24, waiting for transfers between devices, shifted(): lax.ppermute(array, axis, [(i, (i + by) % count) for i in range(count)])  21.1 us
    ppermute x7, starting transfers between devices, summed_over(): lax.ppermute(value, axis, [(i, i ^ step) for i in range(count)])  10.5 us
    pallas_call x1, Pallas kernels, local(): pl.pallas_call(functools.partial(update_kernel, float(tokens * full)), gr...  8.13 us
    ppermute x3, waiting for transfers between devices, local(): hidden = lax.ppermute(result, 'section', [(tick, tick + 1)])  6.87 us
  transfers between devices with their start and end apart: 43, of which 28 were waited for; matrix products, arithmetic and copies ran while one was open for 1% of the time, Pallas kernels for 2%

profile of v2, /device:TPU:5, one launch (start us, length us, event | category | flops | bytes accessed | tf_op | source)
XLA Modules:
  0.0 334.1 jit_solution(1772486846647913694)
XLA Ops:
  5.4 6.8 %shard_map.145 = (bf16[512,2048]{1,0:T(8,128)(2,1)}, bf16[512,512]{1,0:T(8,128)(2,1)}, bf16[512,2560]{1,0:T(8,128)(2,1)S(1)}, bf16[512,2560]{1,0:T(8,128)(2,1)S(1)}) custom-call(s32[5]{0:T(128)S(1)} %stack.61.ints_ref, f32[1]{0:T(128)} %bitcast.16.sign_ref, bf16[512,2048]{1,0:T(8,128)(2,1)} %bitcast.39, bf16[512,512]{1,0:T(8,128)(2,1)} %bitcast.43), custom_call_target="tpu_custom_call" | custom-call | flops 78643200 | bytes 13107200 | tf_op jit(solution)/shard_map/pallas_call | solution.py:293
  12.7 6.0 %shard_map.146 = (bf16[2048,512]{1,0:T(8,128)(2,1)}, bf16[2048,512]{1,0:T(8,128)(2,1)S(1)}, bf16[2048,512]{1,0:T(8,128)(2,1)S(1)}) custom-call(s32[3]{0:T(128)S(1)} %pad_add_fusion.ints_ref, f32[1]{0:T(128)} %bitcast.16.sign_ref, bf16[2048,512]{1,0:T(8,128)(2,1)} %bitcast.41), custom_call_target="tpu_custom_call" | custom-call | flops 62914560 | bytes 10485760 | tf_op jit(solution)/shard_map/pallas_call | solution.py:312
  20.1 2.6 collective-permute-start.3
  27.0 34.3 %all_to_all.40.recv_ref = bf16[8,528,128]{2,1,0:T(8,128)(2,1)S(1)} all-to-all(bf16[8,528,128]{2,1,0:T(8,128)(2,1)S(1)} %shard_map.147), channel_id=1, replica_groups=mesh['section'=4,'y'=4,'z'=8,'core'=2] {'z'}, dimensions={0} | all-to-all | bytes 2162688 | tf_op jit(solution)/shard_map/all_to_all | solution.py:373
  62.5 17.1 %all_to_all.41.heads_ref = bf16[8,256,128]{2,1,0:T(8,128)(2,1)S(1)} all-to-all(bf16[8,256,128]{2,1,0:T(8,128)(2,1)S(1)} %shard_map.148), channel_id=1, replica_groups=mesh['section'=4,'y'=4,'z'=8,'core'=2] {'z'}, dimensions={0} | all-to-all | bytes 1048576 | tf_op jit(solution)/shard_map/all_to_all | solution.py:374
  88.0 2.7 collective-permute-start.12
  94.8 24.3 %all_to_all.42.recv_ref = bf16[8,528,128]{2,1,0:T(8,128)(2,1)S(1)} all-to-all(bf16[8,528,128]{2,1,0:T(8,128)(2,1)S(1)} %shard_map.150), channel_id=1, replica_groups=mesh['section'=4,'y'=4,'z'=8,'core'=2] {'z'}, dimensions={0} | all-to-all | bytes 2162688 | tf_op jit(solution)/shard_map/all_to_all | solution.py:373
  120.3 15.3 %all_to_all.43.heads_ref = bf16[8,256,128]{2,1,0:T(8,128)(2,1)S(1)} all-to-all(bf16[8,256,128]{2,1,0:T(8,128)(2,1)S(1)} %shard_map.151), channel_id=1, replica_groups=mesh['section'=4,'y'=4,'z'=8,'core'=2] {'z'}, dimensions={0} | all-to-all | bytes 1048576 | tf_op jit(solution)/shard_map/all_to_all | solution.py:374
  137.0 2.7 collective-permute-start.15
  144.1 5.6 %collective-permute-done.17.refs_0_.hidden_ref = bf16[2,128,128]{2,1,0:T(8,128)(2,1)S(1)} collective-permute-done((bf16[2,128,128]{2,1,0:T(8,128)(2,1)S(1)}, bf16[2,128,128]{2,1,0:T(8,128)(2,1)S(1)}, u32[]{:S(2)}, u32[]{:S(2)}) %collective-permute-start.17) | collective-permute-done | bytes 65568 | tf_op jit(solution)/shard_map/ppermute | solution.py:382
  157.5 20.5 %all_to_all.44.recv_ref = bf16[8,528,128]{2,1,0:T(8,128)(2,1)S(1)} all-to-all(bf16[8,528,128]{2,1,0:T(8,128)(2,1)S(1)} %shard_map.153), channel_id=1, replica_groups=mesh['section'=4,'y'=4,'z'=8,'core'=2] {'z'}, dimensions={0} | all-to-all | bytes 2162688 | tf_op jit(solution)/shard_map/all_to_all | solution.py:373
  179.2 18.9 %all_to_all.45.heads_ref = bf16[8,256,128]{2,1,0:T(8,128)(2,1)S(1)} all-to-all(bf16[8,256,128]{2,1,0:T(8,128)(2,1)S(1)} %shard_map.154), channel_id=1, replica_groups=mesh['section'=4,'y'=4,'z'=8,'core'=2] {'z'}, dimensions={0} | all-to-all | bytes 1048576 | tf_op jit(solution)/shard_map/all_to_all | solution.py:374
  201.4 9.6 %collective-permute-start.23 = (bf16[2,128,128]{2,1,0:T(8,128)(2,1)S(1)}, bf16[2,128,128]{2,1,0:T(8,128)(2,1)S(1)}, u32[]{:S(2)}, u32[]{:S(2)}) collective-permute-start(bf16[2,128,128]{2,1,0:T(8,128)(2,1)S(1)} %get-tuple-element.71), channel_id=1, source_target_pairs={{0,48},{16,0},{32,16},{48,32},{1,49},{17,1},{33,17},{49,33},{2,50}... | collective-permute-start | bytes 196616 | tf_op jit(solution)/shard_map/ppermute | solution.py:124
  211.1 2.4 collective-permute-done.23
  219.2 2.9 collective-permute-done.25.refs_1_
  223.3 20.5 %all_to_all.46.recv_ref = bf16[8,528,128]{2,1,0:T(8,128)(2,1)S(1)} all-to-all(bf16[8,528,128]{2,1,0:T(8,128)(2,1)S(1)} %shard_map.156), channel_id=1, replica_groups=mesh['section'=4,'y'=4,'z'=8,'core'=2] {'z'}, dimensions={0} | all-to-all | bytes 2162688 | tf_op jit(solution)/shard_map/all_to_all | solution.py:373
  244.9 20.8 %all_to_all.47.heads_ref = bf16[8,256,128]{2,1,0:T(8,128)(2,1)S(1)} all-to-all(bf16[8,256,128]{2,1,0:T(8,128)(2,1)S(1)} %shard_map.157), channel_id=1, replica_groups=mesh['section'=4,'y'=4,'z'=8,'core'=2] {'z'}, dimensions={0} | all-to-all | bytes 1048576 | tf_op jit(solution)/shard_map/all_to_all | solution.py:374
  266.7 3.2 collective-permute-start.29
  273.2 2.8 collective-permute-start.32
  277.2 2.8 collective-permute-done.33
  285.0 3.5 %collective-permute-start.37 = (f32[8,128]{1,0:T(8,128)S(1)}, f32[8,128]{1,0:T(8,128)S(1)}, u32[]{:S(2)}, u32[]{:S(2)}) collective-permute-start(f32[8,128]{1,0:T(8,128)S(1)} %add.127), channel_id=1, source_target_pairs={{0,12},{2,14},{4,8},{6,10},{8,4},{10,6},{12,0},{14,2},{1,13},{3,15... | collective-permute-start | bytes 12296 | tf_op jit(solution)/shard_map/ppermute | solution.py:252
  292.2 27.0 %collective-permute-start.41 = (bf16[128,128]{1,0:T(8,128)(2,1)S(1)}, bf16[128,128]{1,0:T(8,128)(2,1)S(1)}, u32[]{:S(2)}, u32[]{:S(2)}) collective-permute-start(bf16[128,128]{1,0:T(8,128)(2,1)S(1)} %get-tuple-element.91), channel_id=1, source_target_pairs={{0,1},{1,0},{2,3},{3,2},{4,5},{5,4},{6,7},{7,6},{8,9},{9,8},{10,11... | collective-permute-start | bytes 98312 | tf_op jit(solution)/shard_map/ppermute | solution.py:128
  320.7 4.2 %collective-permute-start.42 = (f32[8,128]{1,0:T(8,128)S(1)}, f32[8,128]{1,0:T(8,128)S(1)}, u32[]{:S(2)}, u32[]{:S(2)}) collective-permute-start(f32[8,128]{1,0:T(8,128)S(1)} %add_select_fusion.own_ref), channel_id=1, source_target_pairs={{0,1},{1,0},{2,3},{3,2},{4,5},{5,4},{6,7},{7,6},{8,9},{9,8},{10,11... | collective-permute-start | bytes 12296 | tf_op jit(solution)/shard_map/ppermute | solution.py:128
  325.7 8.1 %shard_map.160 = (bf16[512,2048]{1,0:T(8,128)(2,1)}, bf16[512,512]{1,0:T(8,128)(2,1)}, bf16[2048,512]{1,0:T(8,128)(2,1)}, f32[1,2]{1,0:T(1,128)}, f32[1,8192]{1,0:T(1,128)}) custom-call(s32[1]{0:T(128)} %bitcast.23.core_ref, f32[8,128]{1,0:T(8,128)S(1)} %add_select_fusion.own_ref, f32[8,128]{1,0:T(8,128)S(1)} %collective-permute-done.42.partner_ref, ...), custom_call_target="tpu_custom_call" | custom-call | tf_op jit(solution)/shard_map/pallas_call | solution.py:410
  (115 shorter events, 66.8 us)
Async XLA Ops:
  12.3 11.5 %collective-permute-start.5 = (bf16[512,2560]{1,0:T(8,128)(2,1)S(1)}, bf16[512,2560]{1,0:T(8,128)(2,1)S(1)}, u32[]{:S(2)}, u32[]{:S(2)}) collective-permute-start(bf16[512,2560]{1,0:T(8,128)(2,1)S(1)} %get-tuple-element.52), channel_id=1, source_target_pairs={{0,1},{1,0},{2,3},{3,2},{4,5},{5,4},{6,7},{7,6},{8,9},{9,8},{10,11... | collective-permute-start | bytes 7864328 | tf_op jit(solution)/shard_map/ppermute | solution.py:128
  18.7 5.1 %collective-permute-start.6 = (bf16[2048,512]{1,0:T(8,128)(2,1)S(1)}, bf16[2048,512]{1,0:T(8,128)(2,1)S(1)}, u32[]{:S(2)}, u32[]{:S(2)}) collective-permute-start(bf16[2048,512]{1,0:T(8,128)(2,1)S(1)} %get-tuple-element.55), channel_id=1, source_target_pairs={{0,1},{1,0},{2,3},{3,2},{4,5},{5,4},{6,7},{7,6},{8,9},{9,8},{10,11... | collective-permute-start | bytes 6291464 | tf_op jit(solution)/shard_map/ppermute | solution.py:128
  18.8 5.0 %collective-permute-start.2 = (bf16[2,128,128]{2,1,0:T(8,128)(2,1)S(1)}, bf16[2,128,128]{2,1,0:T(8,128)(2,1)S(1)}, u32[]{:S(2)}, u32[]{:S(2)}) collective-permute-start(bf16[2,128,128]{2,1,0:T(8,128)(2,1)S(1)} %pad_maximum_fusion.refs_0_.hidden_ref), channel_id=1, source_target_pairs={{0,16},{16,32},{32,48},{48,0},{1,17},{17,33},{33,49},{49,1},{2,18}... | collective-permute-start | bytes 196616 | tf_op jit(solution)/shard_map/ppermute | solution.py:124
  20.1 5.5 %collective-permute-start.3 = (bf16[2,128,128]{2,1,0:T(8,128)(2,1)S(1)}, bf16[2,128,128]{2,1,0:T(8,128)(2,1)S(1)}, u32[]{:S(2)}, u32[]{:S(2)}) collective-permute-start(bf16[2,128,128]{2,1,0:T(8,128)(2,1)S(1)} %pad_maximum_fusion.refs_0_.hidden_ref), channel_id=1, source_target_pairs={{0,32},{16,48},{32,0},{48,16},{1,33},{17,49},{33,1},{49,17},{2,34}... | collective-permute-start | bytes 196616 | tf_op jit(solution)/shard_map/ppermute | solution.py:124
  80.5 5.1 %collective-permute-start.7 = (bf16[2,128,128]{2,1,0:T(8,128)(2,1)S(1)}, bf16[2,128,128]{2,1,0:T(8,128)(2,1)S(1)}, u32[]{:S(2)}, u32[]{:S(2)}) collective-permute-start(bf16[2,128,128]{2,1,0:T(8,128)(2,1)S(1)} %get-tuple-element.61), channel_id=1, source_target_pairs={{0,16},{16,32},{32,48},{48,0},{1,17},{17,33},{33,49},{49,1},{2,18}... | collective-permute-start | bytes 196616 | tf_op jit(solution)/shard_map/ppermute | solution.py:124
  80.6 5.0 %collective-permute-start.8 = (bf16[2,128,128]{2,1,0:T(8,128)(2,1)S(1)}, bf16[2,128,128]{2,1,0:T(8,128)(2,1)S(1)}, u32[]{:S(2)}, u32[]{:S(2)}) collective-permute-start(bf16[2,128,128]{2,1,0:T(8,128)(2,1)S(1)} %get-tuple-element.62), channel_id=1, source_target_pairs={{0,32},{16,48},{32,0},{48,16},{1,33},{17,49},{33,1},{49,17},{2,34}... | collective-permute-start | bytes 196616 | tf_op jit(solution)/shard_map/ppermute | solution.py:124
  86.9 4.8 %collective-permute-start.11 = (bf16[2,128,128]{2,1,0:T(8,128)(2,1)S(1)}, bf16[2,128,128]{2,1,0:T(8,128)(2,1)S(1)}, u32[]{:S(2)}, u32[]{:S(2)}) collective-permute-start(bf16[2,128,128]{2,1,0:T(8,128)(2,1)S(1)} %collective-permute-done.10.refs_0_.hidden_ref), channel_id=1, source_target_pairs={{0,16},{16,32},{32,48},{48,0},{1,17},{17,33},{33,49},{49,1},{2,18}... | collective-permute-start | bytes 196616 | tf_op jit(solution)/shard_map/ppermute | solution.py:124
  88.0 5.1 %collective-permute-start.12 = (bf16[2,128,128]{2,1,0:T(8,128)(2,1)S(1)}, bf16[2,128,128]{2,1,0:T(8,128)(2,1)S(1)}, u32[]{:S(2)}, u32[]{:S(2)}) collective-permute-start(bf16[2,128,128]{2,1,0:T(8,128)(2,1)S(1)} %collective-permute-done.10.refs_0_.hidden_ref), channel_id=1, source_target_pairs={{0,32},{16,48},{32,0},{48,16},{1,33},{17,49},{33,1},{49,17},{2,34}... | collective-permute-start | bytes 196616 | tf_op jit(solution)/shard_map/ppermute | solution.py:124
  136.5 4.7 %collective-permute-start.14 = (bf16[2,128,128]{2,1,0:T(8,128)(2,1)S(1)}, bf16[2,128,128]{2,1,0:T(8,128)(2,1)S(1)}, u32[]{:S(2)}, u32[]{:S(2)}) collective-permute-start(bf16[2,128,128]{2,1,0:T(8,128)(2,1)S(1)} %get-tuple-element.65), channel_id=1, source_target_pairs={{0,16},{16,32},{32,48},{48,0},{1,17},{17,33},{33,49},{49,1},{2,18}... | collective-permute-start | bytes 196616 | tf_op jit(solution)/shard_map/ppermute | solution.py:124
  137.0 5.0 %collective-permute-start.15 = (bf16[2,128,128]{2,1,0:T(8,128)(2,1)S(1)}, bf16[2,128,128]{2,1,0:T(8,128)(2,1)S(1)}, u32[]{:S(2)}, u32[]{:S(2)}) collective-permute-start(bf16[2,128,128]{2,1,0:T(8,128)(2,1)S(1)} %get-tuple-element.66), channel_id=1, source_target_pairs={{0,32},{16,48},{32,0},{48,16},{1,33},{17,49},{33,1},{49,17},{2,34}... | collective-permute-start | bytes 196616 | tf_op jit(solution)/shard_map/ppermute | solution.py:124
  142.8 6.9 %collective-permute-start.17 = (bf16[2,128,128]{2,1,0:T(8,128)(2,1)S(1)}, bf16[2,128,128]{2,1,0:T(8,128)(2,1)S(1)}, u32[]{:S(2)}, u32[]{:S(2)}) collective-permute-start(bf16[2,128,128]{2,1,0:T(8,128)(2,1)S(1)} %add_convert_fusion.1), channel_id=1, source_target_pairs={{64,128},{65,129},{66,130},{67,131},{68,132},{69,133},{70,134},{71... | collective-permute-start | bytes 196616 | tf_op jit(solution)/shard_map/ppermute | solution.py:382
  199.0 12.1 %collective-permute-start.21 = (bf16[2,128,128]{2,1,0:T(8,128)(2,1)S(1)}, bf16[2,128,128]{2,1,0:T(8,128)(2,1)S(1)}, u32[]{:S(2)}, u32[]{:S(2)}) collective-permute-start(bf16[2,128,128]{2,1,0:T(8,128)(2,1)S(1)} %get-tuple-element.69), channel_id=1, source_target_pairs={{0,16},{16,32},{32,48},{48,0},{1,17},{17,33},{33,49},{49,1},{2,18}... | collective-permute-start | bytes 196616 | tf_op jit(solution)/shard_map/ppermute | solution.py:124
  199.1 12.0 %collective-permute-start.22 = (bf16[2,128,128]{2,1,0:T(8,128)(2,1)S(1)}, bf16[2,128,128]{2,1,0:T(8,128)(2,1)S(1)}, u32[]{:S(2)}, u32[]{:S(2)}) collective-permute-start(bf16[2,128,128]{2,1,0:T(8,128)(2,1)S(1)} %get-tuple-element.70), channel_id=1, source_target_pairs={{0,32},{16,48},{32,0},{48,16},{1,33},{17,49},{33,1},{49,17},{2,34}... | collective-permute-start | bytes 196616 | tf_op jit(solution)/shard_map/ppermute | solution.py:124
  201.4 12.1 %collective-permute-start.23 = (bf16[2,128,128]{2,1,0:T(8,128)(2,1)S(1)}, bf16[2,128,128]{2,1,0:T(8,128)(2,1)S(1)}, u32[]{:S(2)}, u32[]{:S(2)}) collective-permute-start(bf16[2,128,128]{2,1,0:T(8,128)(2,1)S(1)} %get-tuple-element.71), channel_id=1, source_target_pairs={{0,48},{16,0},{32,16},{48,32},{1,49},{17,1},{33,17},{49,33},{2,50}... | collective-permute-start | bytes 196616 | tf_op jit(solution)/shard_map/ppermute | solution.py:124
  216.2 6.0 %collective-permute-start.25 = (bf16[2,128,128]{2,1,0:T(8,128)(2,1)S(1)}, bf16[2,128,128]{2,1,0:T(8,128)(2,1)S(1)}, u32[]{:S(2)}, u32[]{:S(2)}) collective-permute-start(bf16[2,128,128]{2,1,0:T(8,128)(2,1)S(1)} %collective-permute-done.24.refs_0_.hidden_ref), channel_id=1, source_target_pairs={{0,16},{16,32},{32,48},{48,0},{1,17},{17,33},{33,49},{49,1},{2,18}... | collective-permute-start | bytes 196616 | tf_op jit(solution)/shard_map/ppermute | solution.py:124
  216.8 5.4 %collective-permute-start.26 = (bf16[2,128,128]{2,1,0:T(8,128)(2,1)S(1)}, bf16[2,128,128]{2,1,0:T(8,128)(2,1)S(1)}, u32[]{:S(2)}, u32[]{:S(2)}) collective-permute-start(bf16[2,128,128]{2,1,0:T(8,128)(2,1)S(1)} %collective-permute-done.24.refs_0_.hidden_ref), channel_id=1, source_target_pairs={{0,32},{16,48},{32,0},{48,16},{1,33},{17,49},{33,1},{49,17},{2,34}... | collective-permute-start | bytes 196616 | tf_op jit(solution)/shard_map/ppermute | solution.py:124
  266.7 5.5 %collective-permute-start.29 = (bf16[2,128,128]{2,1,0:T(8,128)(2,1)S(1)}, bf16[2,128,128]{2,1,0:T(8,128)(2,1)S(1)}, u32[]{:S(2)}, u32[]{:S(2)}) collective-permute-start(bf16[2,128,128]{2,1,0:T(8,128)(2,1)S(1)} %get-tuple-element.74), channel_id=1, source_target_pairs={{0,32},{16,48},{32,0},{48,16},{1,33},{17,49},{33,1},{49,17},{2,34}... | collective-permute-start | bytes 196616 | tf_op jit(solution)/shard_map/ppermute | solution.py:124
  282.8 5.7 %collective-permute-start.35 = (f32[8,128]{1,0:T(8,128)S(1)}, f32[8,128]{1,0:T(8,128)S(1)}, u32[]{:S(2)}, u32[]{:S(2)}) collective-permute-start(f32[8,128]{1,0:T(8,128)S(1)} %add.127), channel_id=1, source_target_pairs={{0,4},{2,6},{4,0},{6,2},{8,12},{10,14},{12,8},{14,10},{1,5},{3,7},... | collective-permute-start | bytes 12296 | tf_op jit(solution)/shard_map/ppermute | solution.py:252
  282.9 6.4 %collective-permute-start.36 = (f32[8,128]{1,0:T(8,128)S(1)}, f32[8,128]{1,0:T(8,128)S(1)}, u32[]{:S(2)}, u32[]{:S(2)}) collective-permute-start(f32[8,128]{1,0:T(8,128)S(1)} %add.127), channel_id=1, source_target_pairs={{0,8},{2,10},{4,12},{6,14},{8,0},{10,2},{12,4},{14,6},{1,9},{3,11}... | collective-permute-start | bytes 12296 | tf_op jit(solution)/shard_map/ppermute | solution.py:252
  289.5 29.7 %collective-permute-start.38 = (f32[8,128]{1,0:T(8,128)S(1)}, f32[8,128]{1,0:T(8,128)S(1)}, u32[]{:S(2)}, u32[]{:S(2)}) collective-permute-start(f32[8,128]{1,0:T(8,128)S(1)} %add_add_fusion), channel_id=1, source_target_pairs={{192,0},{193,1},{194,2},{195,3},{196,4},{197,5},{198,6},{199,7},{2... | collective-permute-start | bytes 12296 | tf_op jit(solution)/shard_map/ppermute | solution.py:399
  290.2 29.0 %collective-permute-start.39 = (f32[8,128]{1,0:T(8,128)S(1)}, f32[8,128]{1,0:T(8,128)S(1)}, u32[]{:S(2)}, u32[]{:S(2)}) collective-permute-start(f32[8,128]{1,0:T(8,128)S(1)} %add_add_fusion), channel_id=1, source_target_pairs={{192,64},{193,65},{194,66},{195,67},{196,68},{197,69},{198,70},{19... | collective-permute-start | bytes 12296 | tf_op jit(solution)/shard_map/ppermute | solution.py:399
  290.9 28.3 %collective-permute-start.40 = (f32[8,128]{1,0:T(8,128)S(1)}, f32[8,128]{1,0:T(8,128)S(1)}, u32[]{:S(2)}, u32[]{:S(2)}) collective-permute-start(f32[8,128]{1,0:T(8,128)S(1)} %add_add_fusion), channel_id=1, source_target_pairs={{192,128},{193,129},{194,130},{195,131},{196,132},{197,133},{198,1... | collective-permute-start | bytes 12296 | tf_op jit(solution)/shard_map/ppermute | solution.py:399
  292.2 27.9 %collective-permute-start.41 = (bf16[128,128]{1,0:T(8,128)(2,1)S(1)}, bf16[128,128]{1,0:T(8,128)(2,1)S(1)}, u32[]{:S(2)}, u32[]{:S(2)}) collective-permute-start(bf16[128,128]{1,0:T(8,128)(2,1)S(1)} %get-tuple-element.91), channel_id=1, source_target_pairs={{0,1},{1,0},{2,3},{3,2},{4,5},{5,4},{6,7},{7,6},{8,9},{9,8},{10,11... | collective-permute-start | bytes 98312 | tf_op jit(solution)/shard_map/ppermute | solution.py:128
  320.7 5.0 %collective-permute-start.42 = (f32[8,128]{1,0:T(8,128)S(1)}, f32[8,128]{1,0:T(8,128)S(1)}, u32[]{:S(2)}, u32[]{:S(2)}) collective-permute-start(f32[8,128]{1,0:T(8,128)S(1)} %add_select_fusion.own_ref), channel_id=1, source_target_pairs={{0,1},{1,0},{2,3},{3,2},{4,5},{5,4},{6,7},{7,6},{8,9},{9,8},{10,11... | collective-permute-start | bytes 12296 | tf_op jit(solution)/shard_map/ppermute | solution.py:128
  (22 other events, 193.7 us)

commit v3 on v2

--- a/solution.py
+++ b/solution.py
@@ -70,42 +70,74 @@
     other_ref[...] = (w - shift).astype(jnp.bfloat16)
 
 
-def finish_kernel(base_ref, *refs):
-    pieces = refs[: NY - 1]
-    goal_ref, result_ref, gap_ref = refs[NY - 1 :]
-    total = jnp.zeros(gap_ref.shape, jnp.float32)
+def sum_kernel(base_ref, *refs):
+    pieces, result_ref = refs[:-1], refs[-1]
     for half in range(NC):
         summed = base_ref[half]
         for piece in pieces:
             summed = summed + piece[half].astype(jnp.float32)
-        result = summed.astype(jnp.bfloat16)
-        result_ref[half] = result
-        gap = result.astype(jnp.float32) - goal_ref[half].astype(jnp.float32)
+        result_ref[half] = summed.astype(jnp.bfloat16)
+
+
+def finish_kernel(base_ref, *refs):
+    goals, result_ref, gap_ref = refs[-4:-2], refs[-2], refs[-1]
+    sum_kernel(base_ref, *refs[: NY - 1], result_ref)
+    total = jnp.zeros(gap_ref.shape, jnp.float32)
+    for half, goal_ref in enumerate(goals):
+        gap = result_ref[half].astype(jnp.float32) - goal_ref[...].astype(jnp.float32)
         total = total + jnp.sum((gap * gap).reshape((-1,) + gap_ref.shape), axis=0)
     gap_ref[...] = total
 
 
-def update_kernel(entries, core_ref, own_ref, partner_ref, gain_ref, noise_ref, *refs):
-    rate_ref = refs[-1]
-    loss_ref, new_gain_ref = refs[-3], refs[-2]
-    refs = refs[:-3]
-
-    @pl.when(pl.program_id(0) == 0)
-    def _():
-        own = jnp.sum(own_ref[...]) / entries
-        partner = jnp.sum(partner_ref[...]) / entries
-        first = core_ref[0] == 0
-        plus = jnp.where(first, own, partner)
-        minus = jnp.where(first, partner, own)
-        loss_ref[0, 0] = plus
-        loss_ref[0, 1] = minus
-        rate_ref[0] = learn_rate * ((plus - minus) / (2.0 * perturb_scale))
-        new_gain_ref[...] = gain_ref[...] - rate_ref[0] * noise_ref[...]
-
-    rate = rate_ref[0]
-    count = len(refs) // 3
-    for w_ref, z_ref, out_ref in zip(refs[:count], refs[count : 2 * count], refs[2 * count :]):
-        out_ref[...] = (w_ref[...].astype(jnp.float32) - rate * z_ref[...].astype(jnp.float32)).astype(jnp.bfloat16)
+def update_kernel(
+    entries, chunks, core_ref, own_ref, partner_ref, gain_ref, noise_ref, mine_ref, other_ref, *refs
+):
+    stored, noises, outs = refs[:3], refs[3:6], refs[6:9]
+    loss_ref, new_gain_ref, layer_ref = refs[9:12]
+    held = refs[12:18]
+    made = refs[18:21]
+    load_sems, store_sems = refs[21:]
+
+    def part(ref, chunk):
+        rows = ref.shape[0] // chunks
+        return ref.at[pl.ds(chunk * rows, rows)]
+
+    def load(which, chunk):
+        source = (stored + noises)[which]
+        return pltpu.make_async_copy(
+            part(source, chunk), part(held[which], chunk), load_sems.at[which, chunk]
+        )
+
+    def store(which, chunk):
+        return pltpu.make_async_copy(
+            part(made[which], chunk), part(outs[which], chunk), store_sems.at[which, chunk]
+        )
+
+    for chunk in range(chunks):
+        for which in range(6):
+            load(which, chunk).start()
+    own = jnp.sum(own_ref[...]) / entries
+    partner = jnp.sum(partner_ref[...]) / entries
+    first = core_ref[0] == 0
+    plus = jnp.where(first, own, partner)
+    minus = jnp.where(first, partner, own)
+    loss_ref[0, 0] = plus
+    loss_ref[0, 1] = minus
+    rate = learn_rate * ((plus - minus) / (2.0 * perturb_scale))
+    new_gain_ref[...] = gain_ref[...] - rate * noise_ref[...]
+    layer_ref[0, core_ref[0]] = mine_ref[...]
+    layer_ref[0, 1 - core_ref[0]] = other_ref[...]
+    for chunk in range(chunks):
+        for which in range(3):
+            load(which, chunk).wait()
+            load(3 + which, chunk).wait()
+            w = part(held[which], chunk)[...].astype(jnp.float32)
+            z = part(held[3 + which], chunk)[...].astype(jnp.float32)
+            part(made[which], chunk)[...] = (w - rate * z).astype(jnp.bfloat16)
+            store(which, chunk).start()
+    for chunk in range(chunks):
+        for which in range(3):
+            store(which, chunk).wait()
 
 
 def in_hbm(array):
@@ -285,9 +317,9 @@
     ints = jnp.stack([salt(1), salt(2), block * width, y * query_cols, y * keyval_cols])
     ints_out = jnp.stack([salt(3), y * query_cols, block * width])
     hidden = jnp.stack([inputs, swapped(inputs)])
-    goal = jnp.stack([target, swapped(target)])
-    gains, ints, ints_out, gain_noise, hidden, goal = lax.optimization_barrier(
-        (gains, ints, ints_out, gain_noise, hidden, goal)
+    target_part = swapped(target)
+    gains, ints, ints_out, gain_noise, hidden, target_part = lax.optimization_barrier(
+        (gains, ints, ints_out, gain_noise, hidden, target_part)
     )
     paired = jax.ShapeDtypeStruct((wq.shape[0], query_cols + keyval_cols), jnp.bfloat16)
     zq, zk, in_mine, in_other = pl.pallas_call(
@@ -375,22 +407,26 @@
         base, *pieces = output(heads, hidden)
         pieces = [shifted(piece, "y", NY, k) for k, piece in enumerate(pieces, 1)]
         if tick < 3:
-            for piece in pieces:
-                base = base + piece.astype(jnp.float32)
-            result = base.astype(jnp.bfloat16)
+            result = pl.pallas_call(
+                sum_kernel,
+                in_specs=[VMEM] * NY,
+                out_specs=VMEM,
+                out_shape=jax.ShapeDtypeStruct(hidden.shape, jnp.bfloat16),
+                compiler_params=limit(8),
+            )(base, *pieces)
             record = jnp.where(section == tick, result, record)
             hidden = lax.ppermute(result, "section", [(tick, tick + 1)])
         else:
             result, squared = pl.pallas_call(
                 finish_kernel,
-                in_specs=[VMEM] * (NY + 1),
+                in_specs=[VMEM] * (NY + 2),
                 out_specs=[VMEM] * 2,
                 out_shape=[
                     jax.ShapeDtypeStruct(hidden.shape, jnp.bfloat16),
                     jax.ShapeDtypeStruct((8, LANE), jnp.float32),
                 ],
                 compiler_params=limit(8),
-            )(base, *pieces, goal)
+            )(base, *pieces, target, target_part)
             record = jnp.where(section == tick, result, record)
 
     squared = summed_over(squared, "y", (1, 2, 3))
@@ -399,24 +435,28 @@
     copies = [lax.ppermute(squared, "section", [(sections - 1, k)]) for k in range(sections - 1)]
     squared = jnp.where(section == sections - 1, squared, sum(copies[1:], copies[0]))
     mine, other = record[0], swapped(record[1])
-    layer_outputs = jnp.where(core == 0, jnp.stack([mine, other]), jnp.stack([other, mine]))[None]
-    squared, layer_outputs = lax.optimization_barrier((squared, layer_outputs))
     partner = swapped(squared)
 
     arrays = (wq, wk, wo)
-    specs = [by_rows(w, 8) for w in arrays]
-    tile = pl.BlockSpec((8, LANE), lambda i: (0, 0))
-    line = pl.BlockSpec((1, full), lambda i: (0, 0))
-    new_query, new_keyval, new_output, losses, new_gains = pl.pallas_call(
-        functools.partial(update_kernel, float(tokens * full)),
-        grid=(8,),
-        in_specs=[SMEM, tile, tile, line, line] + specs + specs,
-        out_specs=specs + [SMEM, line],
+    chunks = 4
+    far = pl.BlockSpec(memory_space=pl.ANY)
+    new_query, new_keyval, new_output, losses, new_gains, layer_outputs = pl.pallas_call(
+        functools.partial(update_kernel, float(tokens * full), chunks),
+        in_specs=[SMEM] + [VMEM] * 6 + [far] * 6,
+        out_specs=[far] * 3 + [SMEM] + [VMEM] * 2,
         out_shape=[pltpu.HBM(w.shape, jnp.bfloat16) for w in arrays]
-        + [jax.ShapeDtypeStruct((1, 2), jnp.float32), jax.ShapeDtypeStruct((1, full), jnp.float32)],
-        scratch_shapes=[pltpu.SMEM((1,), jnp.float32)],
-        compiler_params=limit(14),
-    )(core.reshape(1), squared, partner, norm_gains, gain_noise[None], *map(in_hbm, (*arrays, zq, zk, zo)))
+        + [
+            jax.ShapeDtypeStruct((1, 2), jnp.float32),
+            jax.ShapeDtypeStruct((1, full), jnp.float32),
+            jax.ShapeDtypeStruct((1, 2) + mine.shape, jnp.bfloat16),
+        ],
+        scratch_shapes=[pltpu.VMEM(w.shape, jnp.bfloat16) for w in arrays * 3]
+        + [pltpu.SemaphoreType.DMA((6, chunks)), pltpu.SemaphoreType.DMA((3, chunks))],
+        compiler_params=limit(24),
+    )(
+        core.reshape(1), squared, partner, norm_gains, gain_noise[None], mine, other,
+        *map(in_hbm, (*arrays, zq, zk, zo)),
+    )
     return (
         layer_outputs,
         losses,

time: 339 us -> 336 us (level)
    pallas_call x2 -> x5, Pallas kernels: 8.18 us -> 6.72 us  [the longest x1 6.55 us: local(): pl.pallas_call(functools.partial(update_kernel, float(tokens * full), chu...]
  transfers between devices with their start and end apart: 43 -> 43, of which waited for: 28 -> 27; matrix products, arithmetic and copies ran while one was open for 1% -> 1% of each run, Pallas kernels for 2% -> 2%
where the time goes in v3:
time: 336 us; the launch traced here: 332 us
  blocking collectives  172 us (51%)
  starting transfers between devices  90.1 us (27%)
  waiting for transfers between devices  34.5 us (10%)
  Pallas kernels  31.3 us (9%)
    all_to_all x4, blocking collectives, local(): received = lax.all_to_all(project(around), 'z', 0, 0, tiled=True)  99.6 us
    all_to_all x4, blocking collectives, local(): heads = lax.all_to_all(attend(received), 'z', 0, 0, tiled=True)  72.2 us
    ppermute x24, starting transfers between devices, shifted(): lax.ppermute(array, axis, [(i, (i + by) % count) for i in range(count)])  40.3 us
    ppermute x6, starting transfers between devices, swapped(): return lax.ppermute(array, 'core', [(0, 1), (1, 0)])  33.4 us
    ppermute x24, waiting for transfers between devices, shifted(): lax.ppermute(array, axis, [(i, (i + by) % count) for i in range(count)])  20.3 us
    ppermute x7, starting transfers between devices, summed_over(): lax.ppermute(value, axis, [(i, i ^ step) for i in range(count)])  10.5 us
    pallas_call x1, Pallas kernels, local(): pl.pallas_call(functools.partial(perturb_input_kernel, full, spread, NY),...  6.85 us
  transfers between devices with their start and end apart: 43, of which 27 were waited for; matrix products, arithmetic and copies ran while one was open for 1% of the time, Pallas kernels for 2%

profile of v3, /device:TPU:5, one launch (start us, length us, event | category | flops | bytes accessed | tf_op | source)
XLA Modules:
  0.0 332.0 jit_solution(10307609049925752105)
XLA Ops:
  4.6 6.9 %shard_map.145 = (bf16[512,2048]{1,0:T(8,128)(2,1)}, bf16[512,512]{1,0:T(8,128)(2,1)}, bf16[512,2560]{1,0:T(8,128)(2,1)S(1)}, bf16[512,2560]{1,0:T(8,128)(2,1)S(1)}) custom-call(s32[5]{0:T(128)S(1)} %stack.40.ints_ref, f32[1]{0:T(128)} %bitcast.15.sign_ref, bf16[512,2048]{1,0:T(8,128)(2,1)} %bitcast.36, bf16[512,512]{1,0:T(8,128)(2,1)} %bitcast.40), custom_call_target="tpu_custom_call" | custom-call | flops 78643200 | bytes 13107200 | tf_op jit(solution)/shard_map/pallas_call | solution.py:325
  11.9 6.0 %shard_map.146 = (bf16[2048,512]{1,0:T(8,128)(2,1)}, bf16[2048,512]{1,0:T(8,128)(2,1)S(1)}, bf16[2048,512]{1,0:T(8,128)(2,1)S(1)}) custom-call(s32[3]{0:T(128)S(1)} %pad_add_fusion.ints_ref, f32[1]{0:T(128)} %bitcast.15.sign_ref, bf16[2048,512]{1,0:T(8,128)(2,1)} %bitcast.38), custom_call_target="tpu_custom_call" | custom-call | flops 62914560 | bytes 10485760 | tf_op jit(solution)/shard_map/pallas_call | solution.py:344
  19.3 2.6 collective-permute-start.3
  26.3 34.3 %all_to_all.40.recv_ref = bf16[8,528,128]{2,1,0:T(8,128)(2,1)S(1)} all-to-all(bf16[8,528,128]{2,1,0:T(8,128)(2,1)S(1)} %shard_map.147), channel_id=1, replica_groups=mesh['section'=4,'y'=4,'z'=8,'core'=2] {'z'}, dimensions={0} | all-to-all | bytes 2162688 | tf_op jit(solution)/shard_map/all_to_all | solution.py:405
  61.7 17.1 %all_to_all.41.heads_ref = bf16[8,256,128]{2,1,0:T(8,128)(2,1)S(1)} all-to-all(bf16[8,256,128]{2,1,0:T(8,128)(2,1)S(1)} %shard_map.148), channel_id=1, replica_groups=mesh['section'=4,'y'=4,'z'=8,'core'=2] {'z'}, dimensions={0} | all-to-all | bytes 1048576 | tf_op jit(solution)/shard_map/all_to_all | solution.py:406
  87.3 2.7 collective-permute-start.12
  94.1 24.3 %all_to_all.42.recv_ref = bf16[8,528,128]{2,1,0:T(8,128)(2,1)S(1)} all-to-all(bf16[8,528,128]{2,1,0:T(8,128)(2,1)S(1)} %shard_map.151), channel_id=1, replica_groups=mesh['section'=4,'y'=4,'z'=8,'core'=2] {'z'}, dimensions={0} | all-to-all | bytes 2162688 | tf_op jit(solution)/shard_map/all_to_all | solution.py:405
  119.5 15.4 %all_to_all.43.heads_ref = bf16[8,256,128]{2,1,0:T(8,128)(2,1)S(1)} all-to-all(bf16[8,256,128]{2,1,0:T(8,128)(2,1)S(1)} %shard_map.152), channel_id=1, replica_groups=mesh['section'=4,'y'=4,'z'=8,'core'=2] {'z'}, dimensions={0} | all-to-all | bytes 1048576 | tf_op jit(solution)/shard_map/all_to_all | solution.py:406
  136.2 2.7 collective-permute-start.15
  143.4 5.4 %collective-permute-done.17.refs_0_.hidden_ref = bf16[2,128,128]{2,1,0:T(8,128)(2,1)S(1)} collective-permute-done((bf16[2,128,128]{2,1,0:T(8,128)(2,1)S(1)}, bf16[2,128,128]{2,1,0:T(8,128)(2,1)S(1)}, u32[]{:S(2)}, u32[]{:S(2)}) %collective-permute-start.17) | collective-permute-done | bytes 65568 | tf_op jit(solution)/shard_map/ppermute | solution.py:418
  150.2 2.5 collective-permute-start.19
  156.7 20.5 %all_to_all.44.recv_ref = bf16[8,528,128]{2,1,0:T(8,128)(2,1)S(1)} all-to-all(bf16[8,528,128]{2,1,0:T(8,128)(2,1)S(1)} %shard_map.155), channel_id=1, replica_groups=mesh['section'=4,'y'=4,'z'=8,'core'=2] {'z'}, dimensions={0} | all-to-all | bytes 2162688 | tf_op jit(solution)/shard_map/all_to_all | solution.py:405
  178.3 18.9 %all_to_all.45.heads_ref = bf16[8,256,128]{2,1,0:T(8,128)(2,1)S(1)} all-to-all(bf16[8,256,128]{2,1,0:T(8,128)(2,1)S(1)} %shard_map.156), channel_id=1, replica_groups=mesh['section'=4,'y'=4,'z'=8,'core'=2] {'z'}, dimensions={0} | all-to-all | bytes 1048576 | tf_op jit(solution)/shard_map/all_to_all | solution.py:406
  200.7 10.4 %collective-permute-start.23 = (bf16[2,128,128]{2,1,0:T(8,128)(2,1)S(1)}, bf16[2,128,128]{2,1,0:T(8,128)(2,1)S(1)}, u32[]{:S(2)}, u32[]{:S(2)}) collective-permute-start(bf16[2,128,128]{2,1,0:T(8,128)(2,1)S(1)} %get-tuple-element.70), channel_id=1, source_target_pairs={{0,48},{16,0},{32,16},{48,32},{1,49},{17,1},{33,17},{49,33},{2,50}... | collective-permute-start | bytes 196616 | tf_op jit(solution)/shard_map/ppermute | solution.py:156
  216.8 2.4 collective-permute-start.26
  223.3 20.5 %all_to_all.46.recv_ref = bf16[8,528,128]{2,1,0:T(8,128)(2,1)S(1)} all-to-all(bf16[8,528,128]{2,1,0:T(8,128)(2,1)S(1)} %shard_map.159), channel_id=1, replica_groups=mesh['section'=4,'y'=4,'z'=8,'core'=2] {'z'}, dimensions={0} | all-to-all | bytes 2162688 | tf_op jit(solution)/shard_map/all_to_all | solution.py:405
  245.0 20.8 %all_to_all.47.heads_ref = bf16[8,256,128]{2,1,0:T(8,128)(2,1)S(1)} all-to-all(bf16[8,256,128]{2,1,0:T(8,128)(2,1)S(1)} %shard_map.160), channel_id=1, replica_groups=mesh['section'=4,'y'=4,'z'=8,'core'=2] {'z'}, dimensions={0} | all-to-all | bytes 1048576 | tf_op jit(solution)/shard_map/all_to_all | solution.py:406
  266.7 2.5 collective-permute-start.29
  273.2 2.8 collective-permute-start.32
  277.2 2.8 collective-permute-done.33
  285.1 3.5 %collective-permute-start.37 = (f32[8,128]{1,0:T(8,128)S(1)}, f32[8,128]{1,0:T(8,128)S(1)}, u32[]{:S(2)}, u32[]{:S(2)}) collective-permute-start(f32[8,128]{1,0:T(8,128)S(1)} %add.91), channel_id=1, source_target_pairs={{0,12},{2,14},{4,8},{6,10},{8,4},{10,6},{12,0},{14,2},{1,13},{3,15... | collective-permute-start | bytes 12296 | tf_op jit(solution)/shard_map/ppermute | solution.py:284
  292.3 27.0 %collective-permute-start.42 = (bf16[128,128]{1,0:T(8,128)(2,1)S(1)}, bf16[128,128]{1,0:T(8,128)(2,1)S(1)}, u32[]{:S(2)}, u32[]{:S(2)}) collective-permute-start(bf16[128,128]{1,0:T(8,128)(2,1)S(1)} %get-tuple-element.88), channel_id=1, source_target_pairs={{0,1},{1,0},{2,3},{3,2},{4,5},{5,4},{6,7},{7,6},{8,9},{9,8},{10,11... | collective-permute-start | bytes 98312 | tf_op jit(solution)/shard_map/ppermute | solution.py:160
  319.3 5.1 %collective-permute-start.41 = (f32[8,128]{1,0:T(8,128)S(1)}, f32[8,128]{1,0:T(8,128)S(1)}, u32[]{:S(2)}, u32[]{:S(2)}) collective-permute-start(f32[8,128]{1,0:T(8,128)S(1)} %add_select_fusion.own_ref), channel_id=1, source_target_pairs={{0,1},{1,0},{2,3},{3,2},{4,5},{5,4},{6,7},{7,6},{8,9},{9,8},{10,11... | collective-permute-start | bytes 12296 | tf_op jit(solution)/shard_map/ppermute | solution.py:160
  325.2 6.6 %shard_map.163 = (bf16[512,2048]{1,0:T(8,128)(2,1)}, bf16[512,512]{1,0:T(8,128)(2,1)}, bf16[2048,512]{1,0:T(8,128)(2,1)}, f32[1,2]{1,0:T(1,128)}, f32[1,8192]{1,0:T(1,128)}, /*index=5*/bf16[1,2,128,128]{3,2,1,0:T(8,128)(2,1)}) custom-call(s32[1]{0:T(128)} %bitcast.core_ref, f32[8,128]{1,0:T(8,128)S(1)} %add_select_fusion.own_ref, ...), custom_call_target="tpu_custom_call" | custom-call | tf_op jit(solution)/shard_map/pallas_call | solution.py:443
  (115 shorter events, 65.7 us)
Async XLA Ops:
  11.5 11.5 %collective-permute-start.5 = (bf16[512,2560]{1,0:T(8,128)(2,1)S(1)}, bf16[512,2560]{1,0:T(8,128)(2,1)S(1)}, u32[]{:S(2)}, u32[]{:S(2)}) collective-permute-start(bf16[512,2560]{1,0:T(8,128)(2,1)S(1)} %get-tuple-element.51), channel_id=1, source_target_pairs={{0,1},{1,0},{2,3},{3,2},{4,5},{5,4},{6,7},{7,6},{8,9},{9,8},{10,11... | collective-permute-start | bytes 7864328 | tf_op jit(solution)/shard_map/ppermute | solution.py:160
  17.9 5.1 %collective-permute-start.6 = (bf16[2048,512]{1,0:T(8,128)(2,1)S(1)}, bf16[2048,512]{1,0:T(8,128)(2,1)S(1)}, u32[]{:S(2)}, u32[]{:S(2)}) collective-permute-start(bf16[2048,512]{1,0:T(8,128)(2,1)S(1)} %get-tuple-element.54), channel_id=1, source_target_pairs={{0,1},{1,0},{2,3},{3,2},{4,5},{5,4},{6,7},{7,6},{8,9},{9,8},{10,11... | collective-permute-start | bytes 6291464 | tf_op jit(solution)/shard_map/ppermute | solution.py:160
  18.0 5.0 %collective-permute-start.2 = (bf16[2,128,128]{2,1,0:T(8,128)(2,1)S(1)}, bf16[2,128,128]{2,1,0:T(8,128)(2,1)S(1)}, u32[]{:S(2)}, u32[]{:S(2)}) collective-permute-start(bf16[2,128,128]{2,1,0:T(8,128)(2,1)S(1)} %pad_maximum_fusion.refs_0_.hidden_ref), channel_id=1, source_target_pairs={{0,16},{16,32},{32,48},{48,0},{1,17},{17,33},{33,49},{49,1},{2,18}... | collective-permute-start | bytes 196616 | tf_op jit(solution)/shard_map/ppermute | solution.py:156
  19.3 5.5 %collective-permute-start.3 = (bf16[2,128,128]{2,1,0:T(8,128)(2,1)S(1)}, bf16[2,128,128]{2,1,0:T(8,128)(2,1)S(1)}, u32[]{:S(2)}, u32[]{:S(2)}) collective-permute-start(bf16[2,128,128]{2,1,0:T(8,128)(2,1)S(1)} %pad_maximum_fusion.refs_0_.hidden_ref), channel_id=1, source_target_pairs={{0,32},{16,48},{32,0},{48,16},{1,33},{17,49},{33,1},{49,17},{2,34}... | collective-permute-start | bytes 196616 | tf_op jit(solution)/shard_map/ppermute | solution.py:156
  79.7 5.1 %collective-permute-start.7 = (bf16[2,128,128]{2,1,0:T(8,128)(2,1)S(1)}, bf16[2,128,128]{2,1,0:T(8,128)(2,1)S(1)}, u32[]{:S(2)}, u32[]{:S(2)}) collective-permute-start(bf16[2,128,128]{2,1,0:T(8,128)(2,1)S(1)} %get-tuple-element.60), channel_id=1, source_target_pairs={{0,16},{16,32},{32,48},{48,0},{1,17},{17,33},{33,49},{49,1},{2,18}... | collective-permute-start | bytes 196616 | tf_op jit(solution)/shard_map/ppermute | solution.py:156
  79.8 5.0 %collective-permute-start.8 = (bf16[2,128,128]{2,1,0:T(8,128)(2,1)S(1)}, bf16[2,128,128]{2,1,0:T(8,128)(2,1)S(1)}, u32[]{:S(2)}, u32[]{:S(2)}) collective-permute-start(bf16[2,128,128]{2,1,0:T(8,128)(2,1)S(1)} %get-tuple-element.61), channel_id=1, source_target_pairs={{0,32},{16,48},{32,0},{48,16},{1,33},{17,49},{33,1},{49,17},{2,34}... | collective-permute-start | bytes 196616 | tf_op jit(solution)/shard_map/ppermute | solution.py:156
  86.1 4.8 %collective-permute-start.11 = (bf16[2,128,128]{2,1,0:T(8,128)(2,1)S(1)}, bf16[2,128,128]{2,1,0:T(8,128)(2,1)S(1)}, u32[]{:S(2)}, u32[]{:S(2)}) collective-permute-start(bf16[2,128,128]{2,1,0:T(8,128)(2,1)S(1)} %collective-permute-done.10.refs_0_.hidden_ref), channel_id=1, source_target_pairs={{0,16},{16,32},{32,48},{48,0},{1,17},{17,33},{33,49},{49,1},{2,18}... | collective-permute-start | bytes 196616 | tf_op jit(solution)/shard_map/ppermute | solution.py:156
  87.3 5.1 %collective-permute-start.12 = (bf16[2,128,128]{2,1,0:T(8,128)(2,1)S(1)}, bf16[2,128,128]{2,1,0:T(8,128)(2,1)S(1)}, u32[]{:S(2)}, u32[]{:S(2)}) collective-permute-start(bf16[2,128,128]{2,1,0:T(8,128)(2,1)S(1)} %collective-permute-done.10.refs_0_.hidden_ref), channel_id=1, source_target_pairs={{0,32},{16,48},{32,0},{48,16},{1,33},{17,49},{33,1},{49,17},{2,34}... | collective-permute-start | bytes 196616 | tf_op jit(solution)/shard_map/ppermute | solution.py:156
  136.2 5.0 %collective-permute-start.15 = (bf16[2,128,128]{2,1,0:T(8,128)(2,1)S(1)}, bf16[2,128,128]{2,1,0:T(8,128)(2,1)S(1)}, u32[]{:S(2)}, u32[]{:S(2)}) collective-permute-start(bf16[2,128,128]{2,1,0:T(8,128)(2,1)S(1)} %get-tuple-element.65), channel_id=1, source_target_pairs={{0,32},{16,48},{32,0},{48,16},{1,33},{17,49},{33,1},{49,17},{2,34}... | collective-permute-start | bytes 196616 | tf_op jit(solution)/shard_map/ppermute | solution.py:156
  142.1 6.7 %collective-permute-start.17 = (bf16[2,128,128]{2,1,0:T(8,128)(2,1)S(1)}, bf16[2,128,128]{2,1,0:T(8,128)(2,1)S(1)}, u32[]{:S(2)}, u32[]{:S(2)}) collective-permute-start(bf16[2,128,128]{2,1,0:T(8,128)(2,1)S(1)} %shard_map.154), channel_id=1, source_target_pairs={{64,128},{65,129},{66,130},{67,131},{68,132},{69,133},{70,134},{71... | collective-permute-start | bytes 196616 | tf_op jit(solution)/shard_map/ppermute | solution.py:418
  150.2 4.9 %collective-permute-start.19 = (bf16[2,128,128]{2,1,0:T(8,128)(2,1)S(1)}, bf16[2,128,128]{2,1,0:T(8,128)(2,1)S(1)}, u32[]{:S(2)}, u32[]{:S(2)}) collective-permute-start(bf16[2,128,128]{2,1,0:T(8,128)(2,1)S(1)} %collective-permute-done.17.refs_0_.hidden_ref), channel_id=1, source_target_pairs={{0,32},{16,48},{32,0},{48,16},{1,33},{17,49},{33,1},{49,17},{2,34}... | collective-permute-start | bytes 196616 | tf_op jit(solution)/shard_map/ppermute | solution.py:156
  198.2 12.9 %collective-permute-start.21 = (bf16[2,128,128]{2,1,0:T(8,128)(2,1)S(1)}, bf16[2,128,128]{2,1,0:T(8,128)(2,1)S(1)}, u32[]{:S(2)}, u32[]{:S(2)}) collective-permute-start(bf16[2,128,128]{2,1,0:T(8,128)(2,1)S(1)} %get-tuple-element.68), channel_id=1, source_target_pairs={{0,16},{16,32},{32,48},{48,0},{1,17},{17,33},{33,49},{49,1},{2,18}... | collective-permute-start | bytes 196616 | tf_op jit(solution)/shard_map/ppermute | solution.py:156
  198.3 12.8 %collective-permute-start.22 = (bf16[2,128,128]{2,1,0:T(8,128)(2,1)S(1)}, bf16[2,128,128]{2,1,0:T(8,128)(2,1)S(1)}, u32[]{:S(2)}, u32[]{:S(2)}) collective-permute-start(bf16[2,128,128]{2,1,0:T(8,128)(2,1)S(1)} %get-tuple-element.69), channel_id=1, source_target_pairs={{0,32},{16,48},{32,0},{48,16},{1,33},{17,49},{33,1},{49,17},{2,34}... | collective-permute-start | bytes 196616 | tf_op jit(solution)/shard_map/ppermute | solution.py:156
  200.7 12.7 %collective-permute-start.23 = (bf16[2,128,128]{2,1,0:T(8,128)(2,1)S(1)}, bf16[2,128,128]{2,1,0:T(8,128)(2,1)S(1)}, u32[]{:S(2)}, u32[]{:S(2)}) collective-permute-start(bf16[2,128,128]{2,1,0:T(8,128)(2,1)S(1)} %get-tuple-element.70), channel_id=1, source_target_pairs={{0,48},{16,0},{32,16},{48,32},{1,49},{17,1},{33,17},{49,33},{2,50}... | collective-permute-start | bytes 196616 | tf_op jit(solution)/shard_map/ppermute | solution.py:156
  216.8 4.8 %collective-permute-start.26 = (bf16[2,128,128]{2,1,0:T(8,128)(2,1)S(1)}, bf16[2,128,128]{2,1,0:T(8,128)(2,1)S(1)}, u32[]{:S(2)}, u32[]{:S(2)}) collective-permute-start(bf16[2,128,128]{2,1,0:T(8,128)(2,1)S(1)} %collective-permute-done.24.refs_0_.hidden_ref), channel_id=1, source_target_pairs={{0,32},{16,48},{32,0},{48,16},{1,33},{17,49},{33,1},{49,17},{2,34}... | collective-permute-start | bytes 196616 | tf_op jit(solution)/shard_map/ppermute | solution.py:156
  266.6 5.1 %collective-permute-start.28 = (bf16[2,128,128]{2,1,0:T(8,128)(2,1)S(1)}, bf16[2,128,128]{2,1,0:T(8,128)(2,1)S(1)}, u32[]{:S(2)}, u32[]{:S(2)}) collective-permute-start(bf16[2,128,128]{2,1,0:T(8,128)(2,1)S(1)} %get-tuple-element.72), channel_id=1, source_target_pairs={{0,16},{16,32},{32,48},{48,0},{1,17},{17,33},{33,49},{49,1},{2,18}... | collective-permute-start | bytes 196616 | tf_op jit(solution)/shard_map/ppermute | solution.py:156
  266.7 5.0 %collective-permute-start.29 = (bf16[2,128,128]{2,1,0:T(8,128)(2,1)S(1)}, bf16[2,128,128]{2,1,0:T(8,128)(2,1)S(1)}, u32[]{:S(2)}, u32[]{:S(2)}) collective-permute-start(bf16[2,128,128]{2,1,0:T(8,128)(2,1)S(1)} %get-tuple-element.73), channel_id=1, source_target_pairs={{0,32},{16,48},{32,0},{48,16},{1,33},{17,49},{33,1},{49,17},{2,34}... | collective-permute-start | bytes 196616 | tf_op jit(solution)/shard_map/ppermute | solution.py:156
  282.9 5.7 %collective-permute-start.35 = (f32[8,128]{1,0:T(8,128)S(1)}, f32[8,128]{1,0:T(8,128)S(1)}, u32[]{:S(2)}, u32[]{:S(2)}) collective-permute-start(f32[8,128]{1,0:T(8,128)S(1)} %add.91), channel_id=1, source_target_pairs={{0,4},{2,6},{4,0},{6,2},{8,12},{10,14},{12,8},{14,10},{1,5},{3,7},... | collective-permute-start | bytes 12296 | tf_op jit(solution)/shard_map/ppermute | solution.py:284
  282.9 6.4 %collective-permute-start.36 = (f32[8,128]{1,0:T(8,128)S(1)}, f32[8,128]{1,0:T(8,128)S(1)}, u32[]{:S(2)}, u32[]{:S(2)}) collective-permute-start(f32[8,128]{1,0:T(8,128)S(1)} %add.91), channel_id=1, source_target_pairs={{0,8},{2,10},{4,12},{6,14},{8,0},{10,2},{12,4},{14,6},{1,9},{3,11}... | collective-permute-start | bytes 12296 | tf_op jit(solution)/shard_map/ppermute | solution.py:284
  289.6 29.6 %collective-permute-start.38 = (f32[8,128]{1,0:T(8,128)S(1)}, f32[8,128]{1,0:T(8,128)S(1)}, u32[]{:S(2)}, u32[]{:S(2)}) collective-permute-start(f32[8,128]{1,0:T(8,128)S(1)} %add_add_fusion), channel_id=1, source_target_pairs={{192,0},{193,1},{194,2},{195,3},{196,4},{197,5},{198,6},{199,7},{2... | collective-permute-start | bytes 12296 | tf_op jit(solution)/shard_map/ppermute | solution.py:435
  290.3 29.0 %collective-permute-start.39 = (f32[8,128]{1,0:T(8,128)S(1)}, f32[8,128]{1,0:T(8,128)S(1)}, u32[]{:S(2)}, u32[]{:S(2)}) collective-permute-start(f32[8,128]{1,0:T(8,128)S(1)} %add_add_fusion), channel_id=1, source_target_pairs={{192,64},{193,65},{194,66},{195,67},{196,68},{197,69},{198,70},{19... | collective-permute-start | bytes 12296 | tf_op jit(solution)/shard_map/ppermute | solution.py:435
  291.0 28.3 %collective-permute-start.40 = (f32[8,128]{1,0:T(8,128)S(1)}, f32[8,128]{1,0:T(8,128)S(1)}, u32[]{:S(2)}, u32[]{:S(2)}) collective-permute-start(f32[8,128]{1,0:T(8,128)S(1)} %add_add_fusion), channel_id=1, source_target_pairs={{192,128},{193,129},{194,130},{195,131},{196,132},{197,133},{198,1... | collective-permute-start | bytes 12296 | tf_op jit(solution)/shard_map/ppermute | solution.py:435
  292.3 32.9 %collective-permute-start.42 = (bf16[128,128]{1,0:T(8,128)(2,1)S(1)}, bf16[128,128]{1,0:T(8,128)(2,1)S(1)}, u32[]{:S(2)}, u32[]{:S(2)}) collective-permute-start(bf16[128,128]{1,0:T(8,128)(2,1)S(1)} %get-tuple-element.88), channel_id=1, source_target_pairs={{0,1},{1,0},{2,3},{3,2},{4,5},{5,4},{6,7},{7,6},{8,9},{9,8},{10,11... | collective-permute-start | bytes 98312 | tf_op jit(solution)/shard_map/ppermute | solution.py:160
  319.3 5.9 %collective-permute-start.41 = (f32[8,128]{1,0:T(8,128)S(1)}, f32[8,128]{1,0:T(8,128)S(1)}, u32[]{:S(2)}, u32[]{:S(2)}) collective-permute-start(f32[8,128]{1,0:T(8,128)S(1)} %add_select_fusion.own_ref), channel_id=1, source_target_pairs={{0,1},{1,0},{2,3},{3,2},{4,5},{5,4},{6,7},{7,6},{8,9},{9,8},{10,11... | collective-permute-start | bytes 12296 | tf_op jit(solution)/shard_map/ppermute | solution.py:160
  (23 other events, 199.9 us)

commit v4 on v3

--- a/solution.py
+++ b/solution.py
@@ -89,33 +89,35 @@
     gap_ref[...] = total
 
 
+def fetch_kernel(*refs):
+    sems = refs[-1]
+    count = len(refs) // 2
+    copies = [
+        pltpu.make_async_copy(refs[i], refs[count + i], sems.at[i]) for i in range(count)
+    ]
+    for copy in copies:
+        copy.start()
+    for copy in copies:
+        copy.wait()
+
+
 def update_kernel(
     entries, chunks, core_ref, own_ref, partner_ref, gain_ref, noise_ref, mine_ref, other_ref, *refs
 ):
-    stored, noises, outs = refs[:3], refs[3:6], refs[6:9]
+    held, outs = refs[:6], refs[6:9]
     loss_ref, new_gain_ref, layer_ref = refs[9:12]
-    held = refs[12:18]
-    made = refs[18:21]
-    load_sems, store_sems = refs[21:]
+    made = refs[12:15]
+    store_sems = refs[15]
 
     def part(ref, chunk):
         rows = ref.shape[0] // chunks
         return ref.at[pl.ds(chunk * rows, rows)]
-
-    def load(which, chunk):
-        source = (stored + noises)[which]
-        return pltpu.make_async_copy(
-            part(source, chunk), part(held[which], chunk), load_sems.at[which, chunk]
-        )
 
     def store(which, chunk):
         return pltpu.make_async_copy(
             part(made[which], chunk), part(outs[which], chunk), store_sems.at[which, chunk]
         )
 
-    for chunk in range(chunks):
-        for which in range(6):
-            load(which, chunk).start()
     own = jnp.sum(own_ref[...]) / entries
     partner = jnp.sum(partner_ref[...]) / entries
     first = core_ref[0] == 0
@@ -124,17 +126,15 @@
     loss_ref[0, 0] = plus
     loss_ref[0, 1] = minus
     rate = learn_rate * ((plus - minus) / (2.0 * perturb_scale))
-    new_gain_ref[...] = gain_ref[...] - rate * noise_ref[...]
-    layer_ref[0, core_ref[0]] = mine_ref[...]
-    layer_ref[0, 1 - core_ref[0]] = other_ref[...]
     for chunk in range(chunks):
         for which in range(3):
-            load(which, chunk).wait()
-            load(3 + which, chunk).wait()
             w = part(held[which], chunk)[...].astype(jnp.float32)
             z = part(held[3 + which], chunk)[...].astype(jnp.float32)
             part(made[which], chunk)[...] = (w - rate * z).astype(jnp.bfloat16)
             store(which, chunk).start()
+    new_gain_ref[...] = gain_ref[...] - rate * noise_ref[...]
+    layer_ref[0, core_ref[0]] = mine_ref[...]
+    layer_ref[0, 1 - core_ref[0]] = other_ref[...]
     for chunk in range(chunks):
         for which in range(3):
             store(which, chunk).wait()
@@ -432,30 +432,44 @@
     squared = summed_over(squared, "y", (1, 2, 3))
     squared = summed_over(squared, "z", (1,))
     squared = summed_over(squared, "z", (2, 4, 6))
+    arrays = (wq, wk, wo, zq, zk, zo)
+    squared, *arrays = lax.optimization_barrier((squared, *arrays))
+    far = pl.BlockSpec(memory_space=pl.ANY)
+    held = pl.pallas_call(
+        fetch_kernel,
+        in_specs=[far] * 6,
+        out_specs=[VMEM] * 6,
+        out_shape=[pltpu.VMEM(w.shape, jnp.bfloat16) for w in arrays],
+        scratch_shapes=[pltpu.SemaphoreType.DMA((6,))],
+        compiler_params=limit(14),
+        cost_estimate=pl.CostEstimate(
+            flops=0, bytes_accessed=8 * sum(w.size for w in arrays[:3]), transcendentals=0
+        ),
+    )(*map(in_hbm, arrays))
     copies = [lax.ppermute(squared, "section", [(sections - 1, k)]) for k in range(sections - 1)]
     squared = jnp.where(section == sections - 1, squared, sum(copies[1:], copies[0]))
     mine, other = record[0], swapped(record[1])
+    squared, *held = lax.optimization_barrier((squared, *held))
     partner = swapped(squared)
 
-    arrays = (wq, wk, wo)
     chunks = 4
-    far = pl.BlockSpec(memory_space=pl.ANY)
+    held = [pltpu.with_memory_space_constraint(array, pltpu.VMEM) for array in held]
     new_query, new_keyval, new_output, losses, new_gains, layer_outputs = pl.pallas_call(
         functools.partial(update_kernel, float(tokens * full), chunks),
-        in_specs=[SMEM] + [VMEM] * 6 + [far] * 6,
+        in_specs=[SMEM] + [VMEM] * 12,
         out_specs=[far] * 3 + [SMEM] + [VMEM] * 2,
-        out_shape=[pltpu.HBM(w.shape, jnp.bfloat16) for w in arrays]
+        out_shape=[pltpu.HBM(w.shape, jnp.bfloat16) for w in arrays[:3]]
         + [
             jax.ShapeDtypeStruct((1, 2), jnp.float32),
             jax.ShapeDtypeStruct((1, full), jnp.float32),
             jax.ShapeDtypeStruct((1, 2) + mine.shape, jnp.bfloat16),
         ],
-        scratch_shapes=[pltpu.VMEM(w.shape, jnp.bfloat16) for w in arrays * 3]
-        + [pltpu.SemaphoreType.DMA((6, chunks)), pltpu.SemaphoreType.DMA((3, chunks))],
-        compiler_params=limit(24),
+        scratch_shapes=[pltpu.VMEM(w.shape, jnp.bfloat16) for w in arrays[:3]]
+        + [pltpu.SemaphoreType.DMA((3, chunks))],
+        compiler_params=limit(14),
     )(
         core.reshape(1), squared, partner, norm_gains, gain_noise[None], mine, other,
-        *map(in_hbm, (*arrays, zq, zk, zo)),
+        *held,
     )
     return (
         layer_outputs,

time: 336 us -> 335 us (level)
  starting transfers between devices: 90.1 us -> 85 us
    pallas_call x0 -> x1, Pallas kernels: none -> 3.82 us  [local(): pl.pallas_call(fetch_kernel, in_specs=[far] * 6, out_specs=[VMEM] * 6, ou...]
    ppermute x6, starting transfers between devices: 33.4 us -> 29.8 us  [swapped(): return lax.ppermute(array, 'core', [(0, 1), (1, 0)])]
  transfers between devices with their start and end apart: 43 -> 43, of which waited for: 27 -> 27; matrix products, arithmetic and copies ran while one was open for 1% -> 1% of each run, Pallas kernels for 2% -> 3%
where the time goes in v4:
time: 335 us; the launch traced here: 329 us
  blocking collectives  172 us (51%)
  starting transfers between devices  85 us (25%)
  waiting for transfers between devices  34.9 us (10%)
  Pallas kernels  32.8 us (10%)
    all_to_all x4, blocking collectives, local(): received = lax.all_to_all(project(around), 'z', 0, 0, tiled=True)  99.6 us
    all_to_all x4, blocking collectives, local(): heads = lax.all_to_all(attend(received), 'z', 0, 0, tiled=True)  72.2 us
    ppermute x24, starting transfers between devices, shifted(): lax.ppermute(array, axis, [(i, (i + by) % count) for i in range(count)])  38.8 us
    ppermute x6, starting transfers between devices, swapped(): return lax.ppermute(array, 'core', [(0, 1), (1, 0)])  29.8 us
    ppermute x24, waiting for transfers between devices, shifted(): lax.ppermute(array, axis, [(i, (i + by) % count) for i in range(count)])  21.5 us
    ppermute x7, starting transfers between devices, summed_over(): lax.ppermute(value, axis, [(i, i ^ step) for i in range(count)])  10.5 us
    pallas_call x1, Pallas kernels, local(): pl.pallas_call(functools.partial(perturb_input_kernel, full, spread, NY),...  6.84 us
    ppermute x3, waiting for transfers between devices, local(): hidden = lax.ppermute(result, 'section', [(tick, tick + 1)])  6.78 us
  transfers between devices with their start and end apart: 43, of which 27 were waited for; matrix products, arithmetic and copies ran while one was open for 1% of the time, Pallas kernels for 3%

profile of v4, /device:TPU:5, one launch (start us, length us, event | category | flops | bytes accessed | tf_op | source)
XLA Modules:
  0.0 328.8 jit_solution(5306504686478814038)
XLA Ops:
  4.6 6.8 %shard_map.145 = (bf16[512,2048]{1,0:T(8,128)(2,1)}, bf16[512,512]{1,0:T(8,128)(2,1)}, bf16[512,2560]{1,0:T(8,128)(2,1)S(1)}, bf16[512,2560]{1,0:T(8,128)(2,1)S(1)}) custom-call(s32[5]{0:T(128)S(1)} %stack.40.ints_ref, f32[1]{0:T(128)} %bitcast.15.sign_ref, bf16[512,2048]{1,0:T(8,128)(2,1)} %bitcast.36, bf16[512,512]{1,0:T(8,128)(2,1)} %bitcast.40), custom_call_target="tpu_custom_call" | custom-call | flops 78643200 | bytes 13107200 | tf_op jit(solution)/shard_map/pallas_call | solution.py:325
  11.9 6.0 %shard_map.146 = (bf16[2048,512]{1,0:T(8,128)(2,1)}, bf16[2048,512]{1,0:T(8,128)(2,1)S(1)}, bf16[2048,512]{1,0:T(8,128)(2,1)S(1)}) custom-call(s32[3]{0:T(128)S(1)} %pad_add_fusion.ints_ref, f32[1]{0:T(128)} %bitcast.15.sign_ref, bf16[2048,512]{1,0:T(8,128)(2,1)} %bitcast.38), custom_call_target="tpu_custom_call" | custom-call | flops 62914560 | bytes 10485760 | tf_op jit(solution)/shard_map/pallas_call | solution.py:344
  19.3 2.6 collective-permute-start.3
  26.3 34.3 %all_to_all.40.recv_ref = bf16[8,528,128]{2,1,0:T(8,128)(2,1)S(1)} all-to-all(bf16[8,528,128]{2,1,0:T(8,128)(2,1)S(1)} %shard_map.147), channel_id=1, replica_groups=mesh['section'=4,'y'=4,'z'=8,'core'=2] {'z'}, dimensions={0} | all-to-all | bytes 2162688 | tf_op jit(solution)/shard_map/all_to_all | solution.py:405
  61.7 17.1 %all_to_all.41.heads_ref = bf16[8,256,128]{2,1,0:T(8,128)(2,1)S(1)} all-to-all(bf16[8,256,128]{2,1,0:T(8,128)(2,1)S(1)} %shard_map.148), channel_id=1, replica_groups=mesh['section'=4,'y'=4,'z'=8,'core'=2] {'z'}, dimensions={0} | all-to-all | bytes 1048576 | tf_op jit(solution)/shard_map/all_to_all | solution.py:406
  87.3 2.8 collective-permute-start.12
  94.1 24.3 %all_to_all.42.recv_ref = bf16[8,528,128]{2,1,0:T(8,128)(2,1)S(1)} all-to-all(bf16[8,528,128]{2,1,0:T(8,128)(2,1)S(1)} %shard_map.151), channel_id=1, replica_groups=mesh['section'=4,'y'=4,'z'=8,'core'=2] {'z'}, dimensions={0} | all-to-all | bytes 2162688 | tf_op jit(solution)/shard_map/all_to_all | solution.py:405
  119.5 15.5 %all_to_all.43.heads_ref = bf16[8,256,128]{2,1,0:T(8,128)(2,1)S(1)} all-to-all(bf16[8,256,128]{2,1,0:T(8,128)(2,1)S(1)} %shard_map.152), channel_id=1, replica_groups=mesh['section'=4,'y'=4,'z'=8,'core'=2] {'z'}, dimensions={0} | all-to-all | bytes 1048576 | tf_op jit(solution)/shard_map/all_to_all | solution.py:406
  136.2 2.6 collective-permute-start.15
  143.3 5.5 %collective-permute-done.17.refs_0_.hidden_ref = bf16[2,128,128]{2,1,0:T(8,128)(2,1)S(1)} collective-permute-done((bf16[2,128,128]{2,1,0:T(8,128)(2,1)S(1)}, bf16[2,128,128]{2,1,0:T(8,128)(2,1)S(1)}, u32[]{:S(2)}, u32[]{:S(2)}) %collective-permute-start.17) | collective-permute-done | bytes 65568 | tf_op jit(solution)/shard_map/ppermute | solution.py:418
  156.7 20.5 %all_to_all.44.recv_ref = bf16[8,528,128]{2,1,0:T(8,128)(2,1)S(1)} all-to-all(bf16[8,528,128]{2,1,0:T(8,128)(2,1)S(1)} %shard_map.155), channel_id=1, replica_groups=mesh['section'=4,'y'=4,'z'=8,'core'=2] {'z'}, dimensions={0} | all-to-all | bytes 2162688 | tf_op jit(solution)/shard_map/all_to_all | solution.py:405
  178.3 18.9 %all_to_all.45.heads_ref = bf16[8,256,128]{2,1,0:T(8,128)(2,1)S(1)} all-to-all(bf16[8,256,128]{2,1,0:T(8,128)(2,1)S(1)} %shard_map.156), channel_id=1, replica_groups=mesh['section'=4,'y'=4,'z'=8,'core'=2] {'z'}, dimensions={0} | all-to-all | bytes 1048576 | tf_op jit(solution)/shard_map/all_to_all | solution.py:406
  200.8 9.3 %collective-permute-start.23 = (bf16[2,128,128]{2,1,0:T(8,128)(2,1)S(1)}, bf16[2,128,128]{2,1,0:T(8,128)(2,1)S(1)}, u32[]{:S(2)}, u32[]{:S(2)}) collective-permute-start(bf16[2,128,128]{2,1,0:T(8,128)(2,1)S(1)} %get-tuple-element.90), channel_id=1, source_target_pairs={{0,48},{16,0},{32,16},{48,32},{1,49},{17,1},{33,17},{49,33},{2,50}... | collective-permute-start | bytes 196616 | tf_op jit(solution)/shard_map/ppermute | solution.py:156
  210.1 2.6 collective-permute-done.23.refs_2_
  218.2 3.0 collective-permute-done.25.refs_1_
  222.3 20.5 %all_to_all.46.recv_ref = bf16[8,528,128]{2,1,0:T(8,128)(2,1)S(1)} all-to-all(bf16[8,528,128]{2,1,0:T(8,128)(2,1)S(1)} %shard_map.159), channel_id=1, replica_groups=mesh['section'=4,'y'=4,'z'=8,'core'=2] {'z'}, dimensions={0} | all-to-all | bytes 2162688 | tf_op jit(solution)/shard_map/all_to_all | solution.py:405
  244.0 20.7 %all_to_all.47.heads_ref = bf16[8,256,128]{2,1,0:T(8,128)(2,1)S(1)} all-to-all(bf16[8,256,128]{2,1,0:T(8,128)(2,1)S(1)} %shard_map.160), channel_id=1, replica_groups=mesh['section'=4,'y'=4,'z'=8,'core'=2] {'z'}, dimensions={0} | all-to-all | bytes 1048576 | tf_op jit(solution)/shard_map/all_to_all | solution.py:406
  265.9 3.2 collective-permute-start.29
  272.3 2.6 collective-permute-start.32
  276.4 2.5 collective-permute-done.33
  284.0 3.5 %collective-permute-start.37 = (f32[8,128]{1,0:T(8,128)S(1)}, f32[8,128]{1,0:T(8,128)S(1)}, u32[]{:S(2)}, u32[]{:S(2)}) collective-permute-start(f32[8,128]{1,0:T(8,128)S(1)} %add.91), channel_id=1, source_target_pairs={{0,12},{2,14},{4,8},{6,10},{8,4},{10,6},{12,0},{14,2},{1,13},{3,15... | collective-permute-start | bytes 12296 | tf_op jit(solution)/shard_map/ppermute | solution.py:284
  291.2 27.0 %collective-permute-start.42 = (bf16[128,128]{1,0:T(8,128)(2,1)S(1)}, bf16[128,128]{1,0:T(8,128)(2,1)S(1)}, u32[]{:S(2)}, u32[]{:S(2)}) collective-permute-start(bf16[128,128]{1,0:T(8,128)(2,1)S(1)} %get-tuple-element.128), channel_id=1, source_target_pairs={{0,1},{1,0},{2,3},{3,2},{4,5},{5,4},{6,7},{7,6},{8,9},{9,8},{10,11... | collective-permute-start | bytes 98312 | tf_op jit(solution)/shard_map/ppermute | solution.py:160
  318.2 3.8 %shard_map.163 = (bf16[512,2048]{1,0:T(8,128)(2,1)S(1)}, bf16[512,512]{1,0:T(8,128)(2,1)S(1)}, bf16[2048,512]{1,0:T(8,128)(2,1)S(1)}, bf16[512,2048]{1,0:T(8,128...) custom-call(bf16[512,2048]{1,0:T(8,128)(2,1)} %bitcast.37, bf16[512,512]{1,0:T(8,128)(2,1)} %bitcast.41, ...), custom_call_target="tpu_custom_call" | custom-call | bytes 18874368 | tf_op jit(solution)/shard_map/pallas_call | solution.py:438
  324.3 4.2 %shard_map.164 = (bf16[512,2048]{1,0:T(8,128)(2,1)}, bf16[512,512]{1,0:T(8,128)(2,1)}, bf16[2048,512]{1,0:T(8,128)(2,1)}, f32[1,2]{1,0:T(1,128)}, f32[1,8192]{1,0:T(1,128)}, /*index=5*/bf16[1,2,128,128]{3,2,1,0:T(8,128)(2,1)}) custom-call(s32[1]{0:T(128)} %bitcast.core_ref, f32[8,128]{1,0:T(8,128)S(1)} %add_select_fusion.own_ref, ...), custom_call_target="tpu_custom_call" | custom-call | tf_op jit(solution)/shard_map/pallas_call | solution.py:457
  (116 shorter events, 66.3 us)
Async XLA Ops:
  11.5 11.5 %collective-permute-start.5 = (bf16[512,2560]{1,0:T(8,128)(2,1)S(1)}, bf16[512,2560]{1,0:T(8,128)(2,1)S(1)}, u32[]{:S(2)}, u32[]{:S(2)}) collective-permute-start(bf16[512,2560]{1,0:T(8,128)(2,1)S(1)} %get-tuple-element.71), channel_id=1, source_target_pairs={{0,1},{1,0},{2,3},{3,2},{4,5},{5,4},{6,7},{7,6},{8,9},{9,8},{10,11... | collective-permute-start | bytes 7864328 | tf_op jit(solution)/shard_map/ppermute | solution.py:160
  17.9 5.1 %collective-permute-start.6 = (bf16[2048,512]{1,0:T(8,128)(2,1)S(1)}, bf16[2048,512]{1,0:T(8,128)(2,1)S(1)}, u32[]{:S(2)}, u32[]{:S(2)}) collective-permute-start(bf16[2048,512]{1,0:T(8,128)(2,1)S(1)} %get-tuple-element.74), channel_id=1, source_target_pairs={{0,1},{1,0},{2,3},{3,2},{4,5},{5,4},{6,7},{7,6},{8,9},{9,8},{10,11... | collective-permute-start | bytes 6291464 | tf_op jit(solution)/shard_map/ppermute | solution.py:160
  18.0 5.0 %collective-permute-start.2 = (bf16[2,128,128]{2,1,0:T(8,128)(2,1)S(1)}, bf16[2,128,128]{2,1,0:T(8,128)(2,1)S(1)}, u32[]{:S(2)}, u32[]{:S(2)}) collective-permute-start(bf16[2,128,128]{2,1,0:T(8,128)(2,1)S(1)} %pad_maximum_fusion.refs_0_.hidden_ref), channel_id=1, source_target_pairs={{0,16},{16,32},{32,48},{48,0},{1,17},{17,33},{33,49},{49,1},{2,18}... | collective-permute-start | bytes 196616 | tf_op jit(solution)/shard_map/ppermute | solution.py:156
  19.3 5.5 %collective-permute-start.3 = (bf16[2,128,128]{2,1,0:T(8,128)(2,1)S(1)}, bf16[2,128,128]{2,1,0:T(8,128)(2,1)S(1)}, u32[]{:S(2)}, u32[]{:S(2)}) collective-permute-start(bf16[2,128,128]{2,1,0:T(8,128)(2,1)S(1)} %pad_maximum_fusion.refs_0_.hidden_ref), channel_id=1, source_target_pairs={{0,32},{16,48},{32,0},{48,16},{1,33},{17,49},{33,1},{49,17},{2,34}... | collective-permute-start | bytes 196616 | tf_op jit(solution)/shard_map/ppermute | solution.py:156
  79.7 5.1 %collective-permute-start.7 = (bf16[2,128,128]{2,1,0:T(8,128)(2,1)S(1)}, bf16[2,128,128]{2,1,0:T(8,128)(2,1)S(1)}, u32[]{:S(2)}, u32[]{:S(2)}) collective-permute-start(bf16[2,128,128]{2,1,0:T(8,128)(2,1)S(1)} %get-tuple-element.80), channel_id=1, source_target_pairs={{0,16},{16,32},{32,48},{48,0},{1,17},{17,33},{33,49},{49,1},{2,18}... | collective-permute-start | bytes 196616 | tf_op jit(solution)/shard_map/ppermute | solution.py:156
  79.8 5.0 %collective-permute-start.8 = (bf16[2,128,128]{2,1,0:T(8,128)(2,1)S(1)}, bf16[2,128,128]{2,1,0:T(8,128)(2,1)S(1)}, u32[]{:S(2)}, u32[]{:S(2)}) collective-permute-start(bf16[2,128,128]{2,1,0:T(8,128)(2,1)S(1)} %get-tuple-element.81), channel_id=1, source_target_pairs={{0,32},{16,48},{32,0},{48,16},{1,33},{17,49},{33,1},{49,17},{2,34}... | collective-permute-start | bytes 196616 | tf_op jit(solution)/shard_map/ppermute | solution.py:156
  86.1 4.7 %collective-permute-start.11 = (bf16[2,128,128]{2,1,0:T(8,128)(2,1)S(1)}, bf16[2,128,128]{2,1,0:T(8,128)(2,1)S(1)}, u32[]{:S(2)}, u32[]{:S(2)}) collective-permute-start(bf16[2,128,128]{2,1,0:T(8,128)(2,1)S(1)} %collective-permute-done.10.refs_0_.hidden_ref), channel_id=1, source_target_pairs={{0,16},{16,32},{32,48},{48,0},{1,17},{17,33},{33,49},{49,1},{2,18}... | collective-permute-start | bytes 196616 | tf_op jit(solution)/shard_map/ppermute | solution.py:156
  87.3 5.1 %collective-permute-start.12 = (bf16[2,128,128]{2,1,0:T(8,128)(2,1)S(1)}, bf16[2,128,128]{2,1,0:T(8,128)(2,1)S(1)}, u32[]{:S(2)}, u32[]{:S(2)}) collective-permute-start(bf16[2,128,128]{2,1,0:T(8,128)(2,1)S(1)} %collective-permute-done.10.refs_0_.hidden_ref), channel_id=1, source_target_pairs={{0,32},{16,48},{32,0},{48,16},{1,33},{17,49},{33,1},{49,17},{2,34}... | collective-permute-start | bytes 196616 | tf_op jit(solution)/shard_map/ppermute | solution.py:156
  135.8 4.7 %collective-permute-start.14 = (bf16[2,128,128]{2,1,0:T(8,128)(2,1)S(1)}, bf16[2,128,128]{2,1,0:T(8,128)(2,1)S(1)}, u32[]{:S(2)}, u32[]{:S(2)}) collective-permute-start(bf16[2,128,128]{2,1,0:T(8,128)(2,1)S(1)} %get-tuple-element.84), channel_id=1, source_target_pairs={{0,16},{16,32},{32,48},{48,0},{1,17},{17,33},{33,49},{49,1},{2,18}... | collective-permute-start | bytes 196616 | tf_op jit(solution)/shard_map/ppermute | solution.py:156
  136.2 5.1 %collective-permute-start.15 = (bf16[2,128,128]{2,1,0:T(8,128)(2,1)S(1)}, bf16[2,128,128]{2,1,0:T(8,128)(2,1)S(1)}, u32[]{:S(2)}, u32[]{:S(2)}) collective-permute-start(bf16[2,128,128]{2,1,0:T(8,128)(2,1)S(1)} %get-tuple-element.85), channel_id=1, source_target_pairs={{0,32},{16,48},{32,0},{48,16},{1,33},{17,49},{33,1},{49,17},{2,34}... | collective-permute-start | bytes 196616 | tf_op jit(solution)/shard_map/ppermute | solution.py:156
  142.0 6.8 %collective-permute-start.17 = (bf16[2,128,128]{2,1,0:T(8,128)(2,1)S(1)}, bf16[2,128,128]{2,1,0:T(8,128)(2,1)S(1)}, u32[]{:S(2)}, u32[]{:S(2)}) collective-permute-start(bf16[2,128,128]{2,1,0:T(8,128)(2,1)S(1)} %shard_map.154), channel_id=1, source_target_pairs={{64,128},{65,129},{66,130},{67,131},{68,132},{69,133},{70,134},{71... | collective-permute-start | bytes 196616 | tf_op jit(solution)/shard_map/ppermute | solution.py:418
  150.1 4.9 %collective-permute-start.19 = (bf16[2,128,128]{2,1,0:T(8,128)(2,1)S(1)}, bf16[2,128,128]{2,1,0:T(8,128)(2,1)S(1)}, u32[]{:S(2)}, u32[]{:S(2)}) collective-permute-start(bf16[2,128,128]{2,1,0:T(8,128)(2,1)S(1)} %collective-permute-done.17.refs_0_.hidden_ref), channel_id=1, source_target_pairs={{0,32},{16,48},{32,0},{48,16},{1,33},{17,49},{33,1},{49,17},{2,34}... | collective-permute-start | bytes 196616 | tf_op jit(solution)/shard_map/ppermute | solution.py:156
  198.2 11.9 %collective-permute-start.21 = (bf16[2,128,128]{2,1,0:T(8,128)(2,1)S(1)}, bf16[2,128,128]{2,1,0:T(8,128)(2,1)S(1)}, u32[]{:S(2)}, u32[]{:S(2)}) collective-permute-start(bf16[2,128,128]{2,1,0:T(8,128)(2,1)S(1)} %get-tuple-element.88), channel_id=1, source_target_pairs={{0,16},{16,32},{32,48},{48,0},{1,17},{17,33},{33,49},{49,1},{2,18}... | collective-permute-start | bytes 196616 | tf_op jit(solution)/shard_map/ppermute | solution.py:156
  198.3 11.8 %collective-permute-start.22 = (bf16[2,128,128]{2,1,0:T(8,128)(2,1)S(1)}, bf16[2,128,128]{2,1,0:T(8,128)(2,1)S(1)}, u32[]{:S(2)}, u32[]{:S(2)}) collective-permute-start(bf16[2,128,128]{2,1,0:T(8,128)(2,1)S(1)} %get-tuple-element.89), channel_id=1, source_target_pairs={{0,32},{16,48},{32,0},{48,16},{1,33},{17,49},{33,1},{49,17},{2,34}... | collective-permute-start | bytes 196616 | tf_op jit(solution)/shard_map/ppermute | solution.py:156
  200.8 11.9 %collective-permute-start.23 = (bf16[2,128,128]{2,1,0:T(8,128)(2,1)S(1)}, bf16[2,128,128]{2,1,0:T(8,128)(2,1)S(1)}, u32[]{:S(2)}, u32[]{:S(2)}) collective-permute-start(bf16[2,128,128]{2,1,0:T(8,128)(2,1)S(1)} %get-tuple-element.90), channel_id=1, source_target_pairs={{0,48},{16,0},{32,16},{48,32},{1,49},{17,1},{33,17},{49,33},{2,50}... | collective-permute-start | bytes 196616 | tf_op jit(solution)/shard_map/ppermute | solution.py:156
  215.4 5.9 %collective-permute-start.25 = (bf16[2,128,128]{2,1,0:T(8,128)(2,1)S(1)}, bf16[2,128,128]{2,1,0:T(8,128)(2,1)S(1)}, u32[]{:S(2)}, u32[]{:S(2)}) collective-permute-start(bf16[2,128,128]{2,1,0:T(8,128)(2,1)S(1)} %collective-permute-done.24.refs_0_.hidden_ref), channel_id=1, source_target_pairs={{0,16},{16,32},{32,48},{48,0},{1,17},{17,33},{33,49},{49,1},{2,18}... | collective-permute-start | bytes 196616 | tf_op jit(solution)/shard_map/ppermute | solution.py:156
  215.8 5.5 %collective-permute-start.26 = (bf16[2,128,128]{2,1,0:T(8,128)(2,1)S(1)}, bf16[2,128,128]{2,1,0:T(8,128)(2,1)S(1)}, u32[]{:S(2)}, u32[]{:S(2)}) collective-permute-start(bf16[2,128,128]{2,1,0:T(8,128)(2,1)S(1)} %collective-permute-done.24.refs_0_.hidden_ref), channel_id=1, source_target_pairs={{0,32},{16,48},{32,0},{48,16},{1,33},{17,49},{33,1},{49,17},{2,34}... | collective-permute-start | bytes 196616 | tf_op jit(solution)/shard_map/ppermute | solution.py:156
  265.9 5.5 %collective-permute-start.29 = (bf16[2,128,128]{2,1,0:T(8,128)(2,1)S(1)}, bf16[2,128,128]{2,1,0:T(8,128)(2,1)S(1)}, u32[]{:S(2)}, u32[]{:S(2)}) collective-permute-start(bf16[2,128,128]{2,1,0:T(8,128)(2,1)S(1)} %get-tuple-element.93), channel_id=1, source_target_pairs={{0,32},{16,48},{32,0},{48,16},{1,33},{17,49},{33,1},{49,17},{2,34}... | collective-permute-start | bytes 196616 | tf_op jit(solution)/shard_map/ppermute | solution.py:156
  281.8 5.7 %collective-permute-start.35 = (f32[8,128]{1,0:T(8,128)S(1)}, f32[8,128]{1,0:T(8,128)S(1)}, u32[]{:S(2)}, u32[]{:S(2)}) collective-permute-start(f32[8,128]{1,0:T(8,128)S(1)} %add.91), channel_id=1, source_target_pairs={{0,4},{2,6},{4,0},{6,2},{8,12},{10,14},{12,8},{14,10},{1,5},{3,7},... | collective-permute-start | bytes 12296 | tf_op jit(solution)/shard_map/ppermute | solution.py:284
  281.9 6.4 %collective-permute-start.36 = (f32[8,128]{1,0:T(8,128)S(1)}, f32[8,128]{1,0:T(8,128)S(1)}, u32[]{:S(2)}, u32[]{:S(2)}) collective-permute-start(f32[8,128]{1,0:T(8,128)S(1)} %add.91), channel_id=1, source_target_pairs={{0,8},{2,10},{4,12},{6,14},{8,0},{10,2},{12,4},{14,6},{1,9},{3,11}... | collective-permute-start | bytes 12296 | tf_op jit(solution)/shard_map/ppermute | solution.py:284
  288.6 33.5 %collective-permute-start.38 = (f32[8,128]{1,0:T(8,128)S(1)}, f32[8,128]{1,0:T(8,128)S(1)}, u32[]{:S(2)}, u32[]{:S(2)}) collective-permute-start(f32[8,128]{1,0:T(8,128)S(1)} %add_add_fusion), channel_id=1, source_target_pairs={{192,0},{193,1},{194,2},{195,3},{196,4},{197,5},{198,6},{199,7},{2... | collective-permute-start | bytes 12296 | tf_op jit(solution)/shard_map/ppermute | solution.py:449
  289.2 32.8 %collective-permute-start.39 = (f32[8,128]{1,0:T(8,128)S(1)}, f32[8,128]{1,0:T(8,128)S(1)}, u32[]{:S(2)}, u32[]{:S(2)}) collective-permute-start(f32[8,128]{1,0:T(8,128)S(1)} %add_add_fusion), channel_id=1, source_target_pairs={{192,64},{193,65},{194,66},{195,67},{196,68},{197,69},{198,70},{19... | collective-permute-start | bytes 12296 | tf_op jit(solution)/shard_map/ppermute | solution.py:449
  289.9 32.2 %collective-permute-start.40 = (f32[8,128]{1,0:T(8,128)S(1)}, f32[8,128]{1,0:T(8,128)S(1)}, u32[]{:S(2)}, u32[]{:S(2)}) collective-permute-start(f32[8,128]{1,0:T(8,128)S(1)} %add_add_fusion), channel_id=1, source_target_pairs={{192,128},{193,129},{194,130},{195,131},{196,132},{197,133},{198,1... | collective-permute-start | bytes 12296 | tf_op jit(solution)/shard_map/ppermute | solution.py:449
  291.2 33.1 %collective-permute-start.42 = (bf16[128,128]{1,0:T(8,128)(2,1)S(1)}, bf16[128,128]{1,0:T(8,128)(2,1)S(1)}, u32[]{:S(2)}, u32[]{:S(2)}) collective-permute-start(bf16[128,128]{1,0:T(8,128)(2,1)S(1)} %get-tuple-element.128), channel_id=1, source_target_pairs={{0,1},{1,0},{2,3},{3,2},{4,5},{5,4},{6,7},{7,6},{8,9},{9,8},{10,11... | collective-permute-start | bytes 98312 | tf_op jit(solution)/shard_map/ppermute | solution.py:160
  (23 other events, 172.1 us)
